TPU v7x, 256 devices: a whole 4x4x8 slice. The times are simulated.
256 devices in a mesh: blk: 256 (over y, z, x, core).
Axes of the slice: x: 4, y: 4, z: 8, core: 2. Of those that a mesh axis runs over, the one named last changes fastest.
Arguments:
- features: bfloat16 [131072, 8192], P('blk'), may hold values from -600 to 600
- sources: int32 [131072], P('blk'), may hold values from 0 to 3
Outputs:
- similarity: bfloat16 [131072, 6, 512], P('blk')
All inputs are finite; a program needn't handle non-finite values.
Results may differ from a plain program's by a relative error of at most 0.0057.
Values may be sent and summed in bfloat16 or wider, within the bound.
No kernel may reach another device: no remote copies, remote signals or barrier semaphores. Data moves between devices by JAX's collectives and lax.ppermute only.
A program may use at most 128 MiB of HBM per device.

v0:
```python
import jax
import jax.numpy as jnp
from jax import lax
from jax.sharding import PartitionSpec as P

ROUNDS = 3


def passed_along(block, axis, distance):
    devices = range(lax.axis_size(axis))
    route = [((i - distance) % len(devices), i) for i in devices]
    return lax.ppermute(block, axis, route)


def normalize(block):
    squares = jnp.sum(jnp.square(block.astype(jnp.float32)), axis=1, keepdims=True)
    return (block.astype(jnp.float32) / jnp.sqrt(squares + 1e-06)).astype(jnp.bfloat16)


def local(features, sources):
    count = lax.axis_size("blk")
    own_unit = normalize(features)
    held = features
    held_labels = sources
    slots = []
    for step in range(ROUNDS):
        dist = count // 2 - ROUNDS + step
        held, held_labels = passed_along((features, sources), "blk", -dist)
        partner_unit = normalize(held)
        tile = lax.dot_general(
            own_unit, partner_unit, (((1,), (1,)), ((), ())), preferred_element_type=jnp.float32
        )
        same = sources[:, None] == held_labels[None, :]
        forward = jnp.where(same, jnp.float32(0.0), tile).astype(jnp.bfloat16)
        returned = passed_along(forward, "blk", dist)
        slots.append(forward)
        slots.append(returned.T)
    return jnp.stack(slots, axis=1)


def solution(mesh):
    return jax.shard_map(
        local,
        mesh=mesh,
        in_specs=(P("blk", None), P("blk")),
        out_specs=P("blk", None, None),
        check_vma=False,
    )
```

profile of v0, /device:TPU:1, one launch (start us, length us, event | category | flops | bytes accessed | tf_op | source)
XLA Modules:
  0.0 601.7 jit_solution(10819893726916235794)
XLA Ops:
  0.0 6.8 %collective-permute-start.1 = (bf16[512,8192]{1,0:T(8,128)(2,1)}, bf16[512,8192]{1,0:T(8,128)(2,1)}, u32[]{:S(2)}, u32[]{:S(2)}) collective-permute-start(bf16[512,8192]{1,0:T(8,128)(2,1)} %param.2), channel_id=1, source_target_pairs={{125,0},{126,1},{127,2},{128,3},{129,4},{130,5},{131,6},{132,7},{1... | collective-permute-start | bytes 25165832 | tf_op jit(solution)/shard_map/ppermute | solution.py:12
  6.8 2.9 collective-permute-start.7
  9.8 3.1 collective-permute-start
  12.9 3.8 collective-permute-start.3
  16.7 5.1 fusion
  21.9 9.8 %fusion.1 = bf16[512,8192]{1,0:T(8,128)(2,1)} fusion(bf16[512,8192]{1,0:T(8,128)(2,1)} %param.2, f32[512]{0:T(512)S(1)} %add_sqrt_fusion.3), kind=kLoop, calls=%fused_computation.9 | loop fusion | flops 12582912 | bytes 16779264 | tf_op jit(solution)/shard_map/convert_element_type | solution.py:17
  31.7 160.2 %collective-permute-done.1 = bf16[512,8192]{1,0:T(8,128)(2,1)} collective-permute-done((bf16[512,8192]{1,0:T(8,128)(2,1)}, bf16[512,8192]{1,0:T(8,128)(2,1)}, u32[]{:S(2)}, u32[]{:S(2)}) %collective-permute-start.1) | collective-permute-done | bytes 8388640 | tf_op jit(solution)/shard_map/ppermute | solution.py:12
  192.0 82.1 %collective-permute-start.6 = (s32[512]{0:T(512)S(1)}, s32[512]{0:T(512)S(1)}, u32[]{:S(2)}, u32[]{:S(2)}) collective-permute-start(s32[512]{0:T(512)S(1)} %copy-done), channel_id=1, source_target_pairs={{127,0},{128,1},{129,2},{130,3},{131,4},{132,5},{133,6},{134,7},{1... | collective-permute-start | bytes 6152 | tf_op jit(solution)/shard_map/ppermute | solution.py:12
  274.1 5.1 fusion.2
  279.2 91.0 %collective-permute-done.4 = bf16[512,8192]{1,0:T(8,128)(2,1)} collective-permute-done((bf16[512,8192]{1,0:T(8,128)(2,1)}, bf16[512,8192]{1,0:T(8,128)(2,1)}, u32[]{:S(2)}, u32[]{:S(2)}) %collective-permute-start.4) | collective-permute-done | bytes 8388640 | tf_op jit(solution)/shard_map/ppermute | solution.py:12
  370.2 5.1 fusion.4
  375.4 8.4 %fusion.12 = bf16[512,512]{1,0:T(8,128)(2,1)S(1)} fusion(bf16[512,8192]{1,0:T(8,128)(2,1)S(1)} %bitcast.19, bf16[512,8192]{1,0:T(8,128)(2,1)} %collective-permute-done.1, f32[512]{0:T(512)S(1)} %add_sqrt_fusion.2), kind=kOutput, calls=%fused_computation.18 | convolution fusion | flops 4307550208 | bytes 17303552 | tf_op jit(solution)/shard_map/dot_general | solution.py:30
  383.8 8.4 %fusion.10 = bf16[512,512]{1,0:T(8,128)(2,1)S(1)} fusion(bf16[512,8192]{1,0:T(8,128)(2,1)S(1)} %bitcast.19, bf16[512,8192]{1,0:T(8,128)(2,1)} %collective-permute-done.4, f32[512]{0:T(512)S(1)} %add_sqrt_fusion.1), kind=kOutput, calls=%fused_computation.17 | convolution fusion | flops 4307550208 | bytes 17303552 | tf_op jit(solution)/shard_map/dot_general | solution.py:30
  392.2 63.4 %collective-permute-done.7 = bf16[512,8192]{1,0:T(8,128)(2,1)} collective-permute-done((bf16[512,8192]{1,0:T(8,128)(2,1)}, bf16[512,8192]{1,0:T(8,128)(2,1)}, u32[]{:S(2)}, u32[]{:S(2)}) %collective-permute-start.7) | collective-permute-done | bytes 8388640 | tf_op jit(solution)/shard_map/ppermute | solution.py:12
  455.6 5.3 fusion.6
  461.0 9.7 %select_convert_fusion = (bf16[512,512]{1,0:T(8,128)(2,1)}, bf16[512,512]{1,0:T(8,128)(2,1)}, bf16[512,512]{1,0:T(8,128)(2,1)}) fusion(s32[512]{0:T(512)S(1)} %collective-permute-done.6, s32[512]{0:T(512)S(1)} %copy-done, bf16[512,512]{1,0:T(8,128)(2,1)S(1)} %fusion.10, s32[512]{0:T(512)S(1)} %collective-permute-done.3, bf16[512,512]{1,0:T(8,128)(2,1)S(1)} %fusion.12, ...), kind=kOutput, calls=%fused_computation.19 | convolution fusion | flops 4309123072 | bytes 19408896 | tf_op jit(solution)/shard_map/dot_general | solution.py:30
  470.7 97.3 %collective-permute-start.2 = (bf16[512,512]{1,0:T(8,128)(2,1)}, bf16[512,512]{1,0:T(8,128)(2,1)}, u32[]{:S(2)}, u32[]{:S(2)}) collective-permute-start(bf16[512,512]{1,0:T(8,128)(2,1)} %get-tuple-element.7), channel_id=1, source_target_pairs={{131,0},{132,1},{133,2},{134,3},{135,4},{136,5},{137,6},{138,7},{1... | collective-permute-start | bytes 1572872 | tf_op jit(solution)/shard_map/ppermute | solution.py:12
  568.0 2.3 collective-permute-start.5
  570.3 2.1 copy.6
  574.4 4.8 collective-permute-start.8
  579.2 2.1 copy.8
  584.6 4.4 collective-permute-done.5
  591.1 6.7 %collective-permute-done.8 = bf16[512,512]{1,0:T(8,128)(2,1)} collective-permute-done((bf16[512,512]{1,0:T(8,128)(2,1)}, bf16[512,512]{1,0:T(8,128)(2,1)}, u32[]{:S(2)}, u32[]{:S(2)}) %collective-permute-start.8) | collective-permute-done | bytes 524320 | tf_op jit(solution)/shard_map/ppermute | solution.py:12
  598.9 2.8 copy.9
  (23 shorter events, 8.7 us)
Async XLA Ops:
  0.0 192.0 %collective-permute-start.1 = (bf16[512,8192]{1,0:T(8,128)(2,1)}, bf16[512,8192]{1,0:T(8,128)(2,1)}, u32[]{:S(2)}, u32[]{:S(2)}) collective-permute-start(bf16[512,8192]{1,0:T(8,128)(2,1)} %param.2), channel_id=1, source_target_pairs={{125,0},{126,1},{127,2},{128,3},{129,4},{130,5},{131,6},{132,7},{1... | collective-permute-start | bytes 25165832 | tf_op jit(solution)/shard_map/ppermute | solution.py:12
  6.8 363.5 %collective-permute-start.4 = (bf16[512,8192]{1,0:T(8,128)(2,1)}, bf16[512,8192]{1,0:T(8,128)(2,1)}, u32[]{:S(2)}, u32[]{:S(2)}) collective-permute-start(bf16[512,8192]{1,0:T(8,128)(2,1)} %param.2), channel_id=1, source_target_pairs={{126,0},{127,1},{128,2},{129,3},{130,4},{131,5},{132,6},{133,7},{1... | collective-permute-start | bytes 25165832 | tf_op jit(solution)/shard_map/ppermute | solution.py:12
  6.8 448.7 %collective-permute-start.7 = (bf16[512,8192]{1,0:T(8,128)(2,1)}, bf16[512,8192]{1,0:T(8,128)(2,1)}, u32[]{:S(2)}, u32[]{:S(2)}) collective-permute-start(bf16[512,8192]{1,0:T(8,128)(2,1)} %param.2), channel_id=1, source_target_pairs={{127,0},{128,1},{129,2},{130,3},{131,4},{132,5},{133,6},{134,7},{1... | collective-permute-start | bytes 25165832 | tf_op jit(solution)/shard_map/ppermute | solution.py:12
  9.8 451.1 %collective-permute-start = (s32[512]{0:T(512)}, s32[512]{0:T(512)S(1)}, u32[]{:S(2)}, u32[]{:S(2)}) collective-permute-start(s32[512]{0:T(512)} %param.3), channel_id=1, source_target_pairs={{125,0},{126,1},{127,2},{128,3},{129,4},{130,5},{131,6},{132,7},{1... | collective-permute-start | bytes 6152 | tf_op jit(solution)/shard_map/ppermute | solution.py:12
  12.9 448.1 %collective-permute-start.3 = (s32[512]{0:T(512)}, s32[512]{0:T(512)S(1)}, u32[]{:S(2)}, u32[]{:S(2)}) collective-permute-start(s32[512]{0:T(512)} %param.3), channel_id=1, source_target_pairs={{126,0},{127,1},{128,2},{129,3},{130,4},{131,5},{132,6},{133,7},{1... | collective-permute-start | bytes 6152 | tf_op jit(solution)/shard_map/ppermute | solution.py:12
  21.9 170.1 %copy-start = (s32[512]{0:T(512)S(1)}, s32[512]{0:T(512)}, u32[]{:S(2)}) copy-start(s32[512]{0:T(512)} %param.3) | copy-start | bytes 6148
  31.7 343.6 %slice-start = ((s8[8388608]{0:T(1024)(128)(4,1)}), s8[4194304]{0:T(1024)(128)(4,1)S(1)}, s32[]{:S(2)}) async-start(s8[8388608]{0:T(1024)(128)(4,1)} %bitcast.18), calls=%async_computation | async-start | bytes 8388608
  192.0 269.0 %collective-permute-start.6 = (s32[512]{0:T(512)S(1)}, s32[512]{0:T(512)S(1)}, u32[]{:S(2)}, u32[]{:S(2)}) collective-permute-start(s32[512]{0:T(512)S(1)} %copy-done), channel_id=1, source_target_pairs={{127,0},{128,1},{129,2},{130,3},{131,4},{132,5},{133,6},{134,7},{1... | collective-permute-start | bytes 6152 | tf_op jit(solution)/shard_map/ppermute | solution.py:12
  279.2 96.2 %slice-start.1 = ((s8[8388608]{0:T(1024)(128)(4,1)}), s8[4194304]{0:T(1024)(128)(4,1)S(1)}, s32[]{:S(2)}) async-start(s8[8388608]{0:T(1024)(128)(4,1)} %bitcast.18), calls=%async_computation.1 | async-start | bytes 8388608
  470.7 111.7 %collective-permute-start.2 = (bf16[512,512]{1,0:T(8,128)(2,1)}, bf16[512,512]{1,0:T(8,128)(2,1)}, u32[]{:S(2)}, u32[]{:S(2)}) collective-permute-start(bf16[512,512]{1,0:T(8,128)(2,1)} %get-tuple-element.7), channel_id=1, source_target_pairs={{131,0},{132,1},{133,2},{134,3},{135,4},{136,5},{137,6},{138,7},{1... | collective-permute-start | bytes 1572872 | tf_op jit(solution)/shard_map/ppermute | solution.py:12
  568.0 20.9 %collective-permute-start.5 = (bf16[512,512]{1,0:T(8,128)(2,1)}, bf16[512,512]{1,0:T(8,128)(2,1)}, u32[]{:S(2)}, u32[]{:S(2)}) collective-permute-start(bf16[512,512]{1,0:T(8,128)(2,1)} %get-tuple-element.6), channel_id=1, source_target_pairs={{130,0},{131,1},{132,2},{133,3},{134,4},{135,5},{136,6},{137,7},{1... | collective-permute-start | bytes 1572872 | tf_op jit(solution)/shard_map/ppermute | solution.py:12
  574.4 23.4 %collective-permute-start.8 = (bf16[512,512]{1,0:T(8,128)(2,1)}, bf16[512,512]{1,0:T(8,128)(2,1)}, u32[]{:S(2)}, u32[]{:S(2)}) collective-permute-start(bf16[512,512]{1,0:T(8,128)(2,1)} %get-tuple-element.5), channel_id=1, source_target_pairs={{129,0},{130,1},{131,2},{132,3},{133,4},{134,5},{135,6},{136,7},{1... | collective-permute-start | bytes 1572872 | tf_op jit(solution)/shard_map/ppermute | solution.py:12
where the time goes:
time: 610 us; the launch traced here: 602 us
  waiting for transfers between devices  326 us (53%)
  starting transfers between devices  203 us (33%)
  other arithmetic  30.5 us (5%)
  matrix products  26.4 us (4%)
  local copies, waits for them, and re-layouts  15.4 us (3%)
    ppermute x9, waiting for transfers between devices, passed_along(): return lax.ppermute(block, axis, route)  326 us
    ppermute x9, starting transfers between devices, passed_along(): return lax.ppermute(block, axis, route)  203 us
    dot_general x3, matrix products, local(): lax.dot_general(own_unit, partner_unit, (((1,), (1,)), ((), ())), preferr...  26.4 us
    reduce_sum x4, other arithmetic, normalize(): jnp.sum(jnp.square(block.astype(jnp.float32)), axis=1, keepdims=True)  20.6 us
  transfers between devices with their start and end apart: 9, of which 6 were waited for; matrix products, arithmetic and copies ran while one was open for 10% of the time, Pallas kernels for 0%

commit v1 on v0

v1 whole, which is shorter than its diff:
```python
import jax
import jax.numpy as jnp
from jax import lax
from jax.experimental import pallas as pl
from jax.experimental.pallas import tpu as pltpu
from jax.sharding import PartitionSpec as P

N = 256
SEAM = 128
B = 512
HALF = 4096
TAG = 128
WIDE = HALF + TAG
KSTEP = 1024
ROWS = 64
MIB = 1024 * 1024


def send(block, target, only=None):
    pairs = [(i, target(i) % N) for i in range(N) if only is None or only(i)]
    return lax.ppermute(block, "blk", pairs)


def unit_kernel(info, x_ref, tag_ref, keep_ref, other_ref, ahead_ref):
    x = x_ref[...].astype(jnp.float32)
    squares = jnp.sum(x * x, axis=1, keepdims=True)
    unit = (x * (1.0 / jnp.sqrt(squares + 1e-06))).astype(jnp.bfloat16)
    low, high = unit[:, :HALF], unit[:, HALF:]
    tag = tag_ref[...]

    def put(ref, half):
        @pl.when(half == 0)
        def _():
            ref[:, :HALF] = low

        @pl.when(half != 0)
        def _():
            ref[:, :HALF] = high

        ref[:, HALF:] = tag

    put(keep_ref, info[0])
    put(other_ref, 1 - info[0])
    put(ahead_ref, info[1])


def make_units(features, tags, own_half, ahead_half):
    out = jax.ShapeDtypeStruct((B, WIDE), jnp.bfloat16)
    spec = pl.BlockSpec((ROWS, WIDE), lambda r, info: (r, 0))
    return pl.pallas_call(
        unit_kernel,
        out_shape=(out, out, out),
        grid_spec=pltpu.PrefetchScalarGridSpec(
            num_scalar_prefetch=1,
            grid=(B // ROWS,),
            in_specs=[
                pl.BlockSpec((ROWS, 2 * HALF), lambda r, info: (r, 0)),
                pl.BlockSpec((ROWS, TAG), lambda r, info: (r, 0)),
            ],
            out_specs=(spec, spec, spec),
        ),
        compiler_params=pltpu.CompilerParams(vmem_limit_bytes=40 * MIB),
        cost_estimate=pl.CostEstimate(flops=12 * B * HALF, bytes_accessed=20 * MIB, transcendentals=B),
        name="units",
    )(jnp.stack([own_half, ahead_half]).astype(jnp.int32), features, tags)


def tiles(plans, rows, blocks, choices):
    count = len(plans)
    used_rows, used_blocks = len(rows), len(blocks)

    def kernel(info, *refs):
        row_refs = refs[:used_rows]
        block_refs = refs[used_rows : used_rows + used_blocks]
        refs = refs[used_rows + used_blocks :]
        row_tags = refs[:used_rows]
        block_tags = refs[used_rows : used_rows + used_blocks]
        refs = refs[used_rows + used_blocks :]
        out_ref, turned = refs[0], refs[1 : 1 + count]
        total = refs[1 + count]
        step = pl.program_id(0)

        def each(work):
            for t, options in enumerate(plans):
                if len(options) == 1:
                    work(t, options[0][0], options[0][1])
                    continue
                for c, (a, b) in enumerate(options):
                    @pl.when(info[t] == c)
                    def _(t=t, a=a, b=b):
                        work(t, a, b)

        def add(t, a, b):
            part = lax.dot_general(
                row_refs[a][...], block_refs[b][...], (((1,), (1,)), ((), ())), preferred_element_type=jnp.float32
            )

            @pl.when(step == 0)
            def _():
                total[t] = part

            @pl.when(step > 0)
            def _():
                total[t] += part

        each(add)

        @pl.when(step == HALF // KSTEP - 1)
        def _():
            def finish(t, a, b):
                same = lax.dot_general(
                    row_tags[a][...], block_tags[b][...], (((1,), (1,)), ((), ())), preferred_element_type=jnp.float32
                )
                tile = jnp.where(same > 0.5, jnp.float32(0.0), total[t])
                out_ref[t] = tile.astype(jnp.bfloat16)
                turned[t][...] = tile.T.astype(jnp.bfloat16)

            each(finish)

    wide = pl.BlockSpec((B, KSTEP), lambda k, info: (0, k))
    tag = pl.BlockSpec((B, TAG), lambda k, info: (0, HALF // TAG))
    arrays = list(rows) + list(blocks)
    one = jax.ShapeDtypeStruct((B, B), jnp.bfloat16)
    return pl.pallas_call(
        kernel,
        out_shape=(jax.ShapeDtypeStruct((count, B, B), jnp.bfloat16),) + (one,) * count,
        grid_spec=pltpu.PrefetchScalarGridSpec(
            num_scalar_prefetch=1,
            grid=(HALF // KSTEP,),
            in_specs=[wide] * len(arrays) + [tag] * len(arrays),
            out_specs=(pl.BlockSpec((count, B, B), lambda k, info: (0, 0, 0)),)
            + (pl.BlockSpec((B, B), lambda k, info: (0, 0)),) * count,
            scratch_shapes=[pltpu.VMEM((count, B, B), jnp.float32)],
        ),
        compiler_params=pltpu.CompilerParams(vmem_limit_bytes=48 * MIB),
        cost_estimate=pl.CostEstimate(
            flops=2 * count * B * B * HALF, bytes_accessed=4 * MIB * (len(arrays)), transcendentals=0
        ),
        name="tiles",
    )(jnp.stack(choices).astype(jnp.int32), *arrays, *arrays)


def sum_kernel(slots, first, second, third, *refs):
    turned, out_ref = refs[:6], refs[6]
    straight = [first[0], first[1], first[2], second[0], second[1], third[0]]
    for k, back in enumerate((0, 2, 1, 4, 3, 5)):
        both = straight[k].astype(jnp.float32) + turned[back][...].astype(jnp.float32)
        out_ref[slots[k]] = both.astype(jnp.bfloat16)


def add_up(slots, straight, turned):
    whole = pl.BlockSpec(memory_space=pltpu.VMEM)
    return pl.pallas_call(
        sum_kernel,
        out_shape=jax.ShapeDtypeStruct((6, B, B), jnp.bfloat16),
        in_specs=[pl.BlockSpec(memory_space=pltpu.SMEM)] + [whole] * 9,
        out_specs=whole,
        compiler_params=pltpu.CompilerParams(vmem_limit_bytes=40 * MIB),
        cost_estimate=pl.CostEstimate(flops=6 * B * B, bytes_accessed=9 * MIB, transcendentals=0),
        name="add_up",
    )(slots, *straight, *turned)


def local(features, sources):
    me = lax.axis_index("blk")
    odd = me % 2
    place = me % SEAM
    own_half = me // SEAM
    tags = (sources[:, None] == jnp.arange(TAG, dtype=sources.dtype)[None, :]).astype(jnp.bfloat16)
    keep, other, ahead = make_units(features, tags, own_half, ((me - 2) % N) // SEAM)

    opposite = send(other, lambda i: i + SEAM)
    second_half = send(keep, lambda i: i + SEAM, lambda i: i % SEAM < 3)
    after2 = send(ahead, lambda i: i - 2)
    before2 = send(keep, lambda i: i + 2)
    mate = send(keep, lambda i: i ^ 1)
    lone = send(other, lambda i: i - 3, lambda i: i % SEAM == 2)
    after_mate = send(after2, lambda i: i ^ 1)
    before_mate = send(before2, lambda i: i ^ 1)
    before3 = send(before2, lambda i: i + 1, lambda i: i % 2 == 1)
    after3 = send(after2, lambda i: i - 1, lambda i: i % 2 == 0 and i % SEAM != 0)

    zero = jnp.zeros((), jnp.int32)
    near, *near_turned = tiles(
        [[(0, 0)], [(0, 1)], [(0, 2), (1, 2)]],
        [opposite, second_half],
        [mate, after2, before2],
        [zero, zero, place < 2],
    )
    mid, *mid_turned = tiles(
        [[(0, 0)], [(0, 1), (1, 1)]], [opposite, second_half], [after_mate, before_mate], [zero, place < 2]
    )
    far_choice = jnp.where(odd == 1, jnp.where(place == SEAM - 1, 3, 2), jnp.where(place < 3, 1, 0))
    far, *far_turned = tiles(
        [[(0, 0), (1, 0), (0, 1), (0, 2)]], [opposite, second_half], [before3, after3, lone], [far_choice]
    )

    straight = [send(t, lambda i: i + SEAM) for t in (near, mid, far)]
    turned = [
        send(near_turned[0], lambda i: i ^ 1),
        send(near_turned[1], lambda i: i + 2),
        send(near_turned[2], lambda i: i - 2),
        send(mid_turned[0], lambda i: i + 1 if i % 2 else i + 3),
        send(mid_turned[1], lambda i: i - 3 if i % 2 else i - 1),
        send(far_turned[0], lambda i: i + 3 if i % 2 else i - 3),
    ]
    slots = jnp.where(odd == 1, jnp.array([4, 3, 2, 5, 0, 1], jnp.int32), jnp.array([5, 3, 2, 1, 4, 0], jnp.int32))
    return jnp.transpose(add_up(slots, straight, turned), (1, 0, 2))


def solution(mesh):
    return jax.shard_map(
        local,
        mesh=mesh,
        in_specs=(P("blk", None), P("blk")),
        out_specs=P("blk", None, None),
        check_vma=False,
    )
```

time: 610 us -> 524 us (0.86); the launches traced: 602 us -> 524 us
  starting transfers between devices: 203 us -> 78.2 us
  waiting for transfers between devices: 326 us -> 390 us
  Pallas kernels: 0 us -> 50.8 us
  other arithmetic: 30.5 us -> 0.97 us
  matrix products: 26.4 us -> 0 us
  local copies, waits for them, and re-layouts: 15.4 us -> 3.82 us
    ppermute x9 -> x19, starting transfers between devices: 203 us -> 78.2 us  [send(): return lax.ppermute(block, 'blk', pairs)]
    ppermute x9 -> x19, waiting for transfers between devices: 326 us -> 390 us  [send(): return lax.ppermute(block, 'blk', pairs)]
    pallas_call x0 -> x5, Pallas kernels: none -> 50.8 us  [the longest x3 37.2 us: tiles(): pl.pallas_call(kernel, out_shape=(jax.ShapeDtypeStruct((count, B, B), jnp...]
    dot_general x3 -> x0, matrix products: 26.4 us -> none  [local(): lax.dot_general(own_unit, partner_unit, (((1,), (1,)), ((), ())), preferr...]
    reduce_sum x4 -> x0, other arithmetic: 20.6 us -> none  [normalize(): jnp.sum(jnp.square(block.astype(jnp.float32)), axis=1, keepdims=True)]
    another operation x5 -> x1, local copies, waits for them, and re-layouts: 10 us -> 0.07 us  [tiles(): jnp.stack(choices).astype(jnp.int32)]
    convert_element_type x1, other arithmetic: 9.85 us -> 0.81 us  [local(): (sources[:, None] == jnp.arange(TAG, dtype=sources.dtype)[None, :]).astyp...]
  transfers between devices with their start and end apart: 9 -> 19, of which waited for: 6 -> 4; matrix products, arithmetic and copies ran while one was open for 10% -> 0% of each run, Pallas kernels for 0% -> 7%
where the time goes in v1:
time: 524 us
  waiting for transfers between devices  390 us (74%)
  starting transfers between devices  78.2 us (15%)
  Pallas kernels  50.8 us (10%)
    ppermute x19, waiting for transfers between devices, send(): return lax.ppermute(block, 'blk', pairs)  390 us
    ppermute x19, starting transfers between devices, send(): return lax.ppermute(block, 'blk', pairs)  78.2 us
    pallas_call x3, Pallas kernels, tiles(): pl.pallas_call(kernel, out_shape=(jax.ShapeDtypeStruct((count, B, B), jnp...  37.2 us
  transfers between devices with their start and end apart: 19, of which 4 were waited for; matrix products, arithmetic and copies ran while one was open for 0% of the time, Pallas kernels for 7%

profile of v1, /device:TPU:1, one launch (start us, length us, event | category | flops | bytes accessed | tf_op | source)
XLA Modules:
  0.0 523.9 jit_solution(13057612509105638326)
XLA Ops:
  0.9 9.9 %units.1 = (bf16[512,4224]{1,0:T(8,128)(2,1)S(1)}, bf16[512,4224]{1,0:T(8,128)(2,1)}, bf16[512,4224]{1,0:T(8,128)(2,1)S(1)}) custom-call(s32[2]{0:T(128)S(1)} %pad_add_fusion.info, bf16[512,8192]{1,0:T(8,128)(2,1)} %x_ref.1, bf16[512,128]{1,0:T(8,128)(2,1)S(1)} %fusion.tag_ref), custom_call_target="tpu_custom_call" | custom-call | flops 25165824 | bytes 20971520 | tf_op jit(solution)/shard_map/units/pallas_call | solution.py:50
  10.9 3.7 collective-permute-start
  14.6 8.3 %collective-permute-start.3 = (bf16[512,4224]{1,0:T(8,128)(2,1)S(1)}, bf16[512,4224]{1,0:T(8,128)(2,1)}, u32[]{:S(2)}, u32[]{:S(2)}) collective-permute-start(bf16[512,4224]{1,0:T(8,128)(2,1)S(1)} %get-tuple-element.19), channel_id=1, source_target_pairs={{0,254},{1,255},{2,0},{3,1},{4,2},{5,3},{6,4},{7,5},{8,6},{9,7},{1... | collective-permute-start | bytes 12976136 | tf_op jit(solution)/shard_map/ppermute | solution.py:21
  22.8 3.3 collective-permute-start.1
  26.2 1.6 collective-permute-start.2
  27.8 246.9 %collective-permute-done.refs_0_.refs_5_.refs_4_ = bf16[512,4224]{1,0:T(8,128)(2,1)} collective-permute-done((bf16[512,4224]{1,0:T(8,128)(2,1)}, bf16[512,4224]{1,0:T(8,128)(2,1)}, u32[]{:S(2)}, u32[]{:S(2)}) %collective-permute-start) | collective-permute-done | bytes 4325408 | tf_op jit(solution)/shard_map/ppermute | solution.py:21
  274.7 2.7 collective-permute-start.11
  277.4 6.4 %collective-permute-start.6 = (bf16[512,4224]{1,0:T(8,128)(2,1)}, bf16[512,4224]{1,0:T(8,128)(2,1)}, u32[]{:S(2)}, u32[]{:S(2)}) collective-permute-start(bf16[512,4224]{1,0:T(8,128)(2,1)} %collective-permute-done.3.refs_3_.refs_8_), channel_id=1, source_target_pairs={{0,1},{1,0},{2,3},{3,2},{4,5},{5,4},{6,7},{7,6},{8,9},{9,8},{10,11... | collective-permute-start | bytes 12976136 | tf_op jit(solution)/shard_map/ppermute | solution.py:21
  283.9 83.4 %collective-permute-done.1.refs_1_.refs_6_.refs_5_ = bf16[512,4224]{1,0:T(8,128)(2,1)S(1)} collective-permute-done((bf16[512,4224]{1,0:T(8,128)(2,1)S(1)}, bf16[512,4224]{1,0:T(8,128)(2,1)S(1)}, u32[]{:S(2)}, u32[]{:S(2)}) %collective-permute-start.1) | collective-permute-done | bytes 4325408 | tf_op jit(solution)/shard_map/ppermute | solution.py:21
  367.3 3.3 collective-permute-start.9
  370.6 2.1 copy-done.5
  374.1 16.0 %tiles.3 = (bf16[3,512,512]{2,1,0:T(8,128)(2,1)}, bf16[512,512]{1,0:T(8,128)(2,1)}, bf16[512,512]{1,0:T(8,128)(2,1)}, bf16[512,512]{1,0:T(8,128)(2,1)}) custom-call(s32[3]{0:T(128)S(1)} %stack.27.info, bf16[512,4224]{1,0:T(8,128)(2,1)} %collective-permute-done.refs_0_.refs_5_.refs_4_, bf16[512,4224]{1,0:T(8,128)(2,1)} %copy-done.4, ...), custom_call_target="tpu_custom_call" | custom-call | flops 6442450944 | bytes 20971520 | tf_op jit(solution)/shard_map/tiles/pallas_call | solution.py:124
  390.2 3.1 collective-permute-start.5
  393.4 1.9 collective-permute-start.13
  395.3 2.9 collective-permute-start.14
  398.3 23.1 %collective-permute-done.9.refs_2_.refs_7_ = bf16[512,4224]{1,0:T(8,128)(2,1)} collective-permute-done((bf16[512,4224]{1,0:T(8,128)(2,1)}, bf16[512,4224]{1,0:T(8,128)(2,1)}, u32[]{:S(2)}, u32[]{:S(2)}) %collective-permute-start.9) | collective-permute-done | bytes 4325408 | tf_op jit(solution)/shard_map/ppermute | solution.py:21
  421.4 29.2 %collective-permute-start.15 = (bf16[512,512]{1,0:T(8,128)(2,1)}, bf16[512,512]{1,0:T(8,128)(2,1)}, u32[]{:S(2)}, u32[]{:S(2)}) collective-permute-start(bf16[512,512]{1,0:T(8,128)(2,1)} %get-tuple-element.25), channel_id=1, source_target_pairs={{0,254},{1,255},{2,0},{3,1},{4,2},{5,3},{6,4},{7,5},{8,6},{9,7},{1... | collective-permute-start | bytes 1572872 | tf_op jit(solution)/shard_map/ppermute | solution.py:21
  450.6 12.0 %tiles.4 = (bf16[2,512,512]{2,1,0:T(8,128)(2,1)}, bf16[512,512]{1,0:T(8,128)(2,1)S(1)}, bf16[512,512]{1,0:T(8,128)(2,1)S(1)}) custom-call(s32[2]{0:T(128)S(1)} %pad_add_fusion.1.info, bf16[512,4224]{1,0:T(8,128)(2,1)} %collective-permute-done.refs_0_.refs_5_.refs_4_, bf16[512,4224]{1,0:T(8,128)(2,1)} %copy-done.4, ...), custom_call_target="tpu_custom_call" | custom-call | flops 4294967296 | bytes 16777216 | tf_op jit(solution)/shard_map/tiles/pallas_call | solution.py:124
  464.2 9.2 %tiles.5 = (bf16[1,512,512]{2,1,0:T(8,128)(2,1)S(1)}, bf16[512,512]{1,0:T(8,128)(2,1)S(1)}) custom-call(s32[1]{0:T(128)} %bitcast.3.info, bf16[512,4224]{1,0:T(8,128)(2,1)} %collective-permute-done.refs_0_.refs_5_.refs_4_, bf16[512,4224]{1,0:T(8,128)(2,1)} %copy-done.4, bf16[512,4224]{1,0:T(8,128)(2,1)} %collective-permute-done.9.refs_2_.refs_7_, ...), custom_call_target="tpu_custom_call" | custom-call | flops 2147483648 | bytes 20971520 | tf_op jit(solution)/shard_map/tiles/pallas_call | solution.py:124
  473.4 3.0 collective-permute-start.12
  476.4 5.8 %collective-permute-start.16 = (bf16[512,512]{1,0:T(8,128)(2,1)S(1)}, bf16[512,512]{1,0:T(8,128)(2,1)S(1)}, u32[]{:S(2)}, u32[]{:S(2)}) collective-permute-start(bf16[512,512]{1,0:T(8,128)(2,1)S(1)} %copy-done.3), channel_id=1, source_target_pairs={{0,3},{1,2},{2,5},{3,4},{4,7},{5,6},{6,9},{7,8},{8,11},{9,10},{10,... | collective-permute-start | bytes 1572872 | tf_op jit(solution)/shard_map/ppermute | solution.py:21
  482.2 1.4 collective-permute-start.17
  483.7 36.6 %collective-permute-done.12.third = bf16[1,512,512]{2,1,0:T(8,128)(2,1)S(1)} collective-permute-done((bf16[1,512,512]{2,1,0:T(8,128)(2,1)S(1)}, bf16[1,512,512]{2,1,0:T(8,128)(2,1)S(1)}, u32[]{:S(2)}, u32[]{:S(2)}) %collective-permute-start.12) | collective-permute-done | bytes 524320 | tf_op jit(solution)/shard_map/ppermute | solution.py:21
  520.3 3.6 add_up.1
  (40 shorter events, 4.1 us)
Async XLA Ops:
  10.9 263.9 %collective-permute-start = (bf16[512,4224]{1,0:T(8,128)(2,1)}, bf16[512,4224]{1,0:T(8,128)(2,1)}, u32[]{:S(2)}, u32[]{:S(2)}) collective-permute-start(bf16[512,4224]{1,0:T(8,128)(2,1)} %get-tuple-element.17), channel_id=1, source_target_pairs={{0,128},{1,129},{2,130},{3,131},{4,132},{5,133},{6,134},{7,135},{8... | collective-permute-start | bytes 12976136 | tf_op jit(solution)/shard_map/ppermute | solution.py:21
  14.6 262.9 %collective-permute-start.3 = (bf16[512,4224]{1,0:T(8,128)(2,1)S(1)}, bf16[512,4224]{1,0:T(8,128)(2,1)}, u32[]{:S(2)}, u32[]{:S(2)}) collective-permute-start(bf16[512,4224]{1,0:T(8,128)(2,1)S(1)} %get-tuple-element.19), channel_id=1, source_target_pairs={{0,254},{1,255},{2,0},{3,1},{4,2},{5,3},{6,4},{7,5},{8,6},{9,7},{1... | collective-permute-start | bytes 12976136 | tf_op jit(solution)/shard_map/ppermute | solution.py:21
  22.8 261.0 %collective-permute-start.4 = (bf16[512,4224]{1,0:T(8,128)(2,1)S(1)}, bf16[512,4224]{1,0:T(8,128)(2,1)}, u32[]{:S(2)}, u32[]{:S(2)}) collective-permute-start(bf16[512,4224]{1,0:T(8,128)(2,1)S(1)} %get-tuple-element.18), channel_id=1, source_target_pairs={{0,2},{1,3},{2,4},{3,5},{4,6},{5,7},{6,8},{7,9},{8,10},{9,11},{10,... | collective-permute-start | bytes 12976136 | tf_op jit(solution)/shard_map/ppermute | solution.py:21
  22.8 344.4 %collective-permute-start.1 = (bf16[512,4224]{1,0:T(8,128)(2,1)S(1)}, bf16[512,4224]{1,0:T(8,128)(2,1)S(1)}, u32[]{:S(2)}, u32[]{:S(2)}) collective-permute-start(bf16[512,4224]{1,0:T(8,128)(2,1)S(1)} %get-tuple-element.18), channel_id=1, source_target_pairs={{0,128},{1,129},{2,130},{128,0},{129,1},{130,2}} | collective-permute-start | bytes 12976136 | tf_op jit(solution)/shard_map/ppermute | solution.py:21
  26.2 344.5 %collective-permute-start.2 = (bf16[512,4224]{1,0:T(8,128)(2,1)S(1)}, bf16[512,4224]{1,0:T(8,128)(2,1)S(1)}, u32[]{:S(2)}, u32[]{:S(2)}) collective-permute-start(bf16[512,4224]{1,0:T(8,128)(2,1)S(1)} %get-tuple-element.18), channel_id=1, source_target_pairs={{0,1},{1,0},{2,3},{3,2},{4,5},{5,4},{6,7},{7,6},{8,9},{9,8},{10,11... | collective-permute-start | bytes 12976136 | tf_op jit(solution)/shard_map/ppermute | solution.py:21
  274.7 115.5 %collective-permute-start.11 = (bf16[512,4224]{1,0:T(8,128)(2,1)}, bf16[512,4224]{1,0:T(8,128)(2,1)}, u32[]{:S(2)}, u32[]{:S(2)}) collective-permute-start(bf16[512,4224]{1,0:T(8,128)(2,1)} %get-tuple-element.17), channel_id=1, source_target_pairs={{2,255},{130,127}} | collective-permute-start | bytes 12976136 | tf_op jit(solution)/shard_map/ppermute | solution.py:21
  277.4 116.0 %collective-permute-start.6 = (bf16[512,4224]{1,0:T(8,128)(2,1)}, bf16[512,4224]{1,0:T(8,128)(2,1)}, u32[]{:S(2)}, u32[]{:S(2)}) collective-permute-start(bf16[512,4224]{1,0:T(8,128)(2,1)} %collective-permute-done.3.refs_3_.refs_8_), channel_id=1, source_target_pairs={{0,1},{1,0},{2,3},{3,2},{4,5},{5,4},{6,7},{7,6},{8,9},{9,8},{10,11... | collective-permute-start | bytes 12976136 | tf_op jit(solution)/shard_map/ppermute | solution.py:21
  283.8 111.5 %collective-permute-start.7 = (bf16[512,4224]{1,0:T(8,128)(2,1)}, bf16[512,4224]{1,0:T(8,128)(2,1)}, u32[]{:S(2)}, u32[]{:S(2)}) collective-permute-start(bf16[512,4224]{1,0:T(8,128)(2,1)} %collective-permute-done.4.refs_4_.refs_9_), channel_id=1, source_target_pairs={{0,1},{1,0},{2,3},{3,2},{4,5},{5,4},{6,7},{7,6},{8,9},{9,8},{10,11... | collective-permute-start | bytes 12976136 | tf_op jit(solution)/shard_map/ppermute | solution.py:21
  367.3 3.3 copy-start.4
  367.3 54.1 %collective-permute-start.9 = (bf16[512,4224]{1,0:T(8,128)(2,1)}, bf16[512,4224]{1,0:T(8,128)(2,1)}, u32[]{:S(2)}, u32[]{:S(2)}) collective-permute-start(bf16[512,4224]{1,0:T(8,128)(2,1)} %collective-permute-done.4.refs_4_.refs_9_), channel_id=1, source_target_pairs={{1,2},{3,4},{5,6},{7,8},{9,10},{11,12},{13,14},{15,16},{17,18},{19... | collective-permute-start | bytes 12976136 | tf_op jit(solution)/shard_map/ppermute | solution.py:21
  372.8 91.4 %collective-permute-start.10 = (bf16[512,4224]{1,0:T(8,128)(2,1)}, bf16[512,4224]{1,0:T(8,128)(2,1)}, u32[]{:S(2)}, u32[]{:S(2)}) collective-permute-start(bf16[512,4224]{1,0:T(8,128)(2,1)} %collective-permute-done.3.refs_3_.refs_8_), channel_id=1, source_target_pairs={{2,1},{4,3},{6,5},{8,7},{10,9},{12,11},{14,13},{16,15},{18,17},{20... | collective-permute-start | bytes 12976136 | tf_op jit(solution)/shard_map/ppermute | solution.py:21
  390.2 93.4 %collective-permute-start.5 = (bf16[3,512,512]{2,1,0:T(8,128)(2,1)}, bf16[3,512,512]{2,1,0:T(8,128)(2,1)S(1)}, u32[]{:S(2)}, u32[]{:S(2)}) collective-permute-start(bf16[3,512,512]{2,1,0:T(8,128)(2,1)} %get-tuple-element.20), channel_id=1, source_target_pairs={{0,128},{1,129},{2,130},{3,131},{4,132},{5,133},{6,134},{7,135},{8... | collective-permute-start | bytes 4718600 | tf_op jit(solution)/shard_map/ppermute | solution.py:21
  393.4 80.0 %collective-permute-start.13 = (bf16[512,512]{1,0:T(8,128)(2,1)}, bf16[512,512]{1,0:T(8,128)(2,1)S(1)}, u32[]{:S(2)}, u32[]{:S(2)}) collective-permute-start(bf16[512,512]{1,0:T(8,128)(2,1)} %get-tuple-element.23), channel_id=1, source_target_pairs={{0,1},{1,0},{2,3},{3,2},{4,5},{5,4},{6,7},{7,6},{8,9},{9,8},{10,11... | collective-permute-start | bytes 1572872 | tf_op jit(solution)/shard_map/ppermute | solution.py:21
  395.3 81.1 %collective-permute-start.14 = (bf16[512,512]{1,0:T(8,128)(2,1)}, bf16[512,512]{1,0:T(8,128)(2,1)}, u32[]{:S(2)}, u32[]{:S(2)}) collective-permute-start(bf16[512,512]{1,0:T(8,128)(2,1)} %get-tuple-element.24), channel_id=1, source_target_pairs={{0,2},{1,3},{2,4},{3,5},{4,6},{5,7},{6,8},{7,9},{8,10},{9,11},{10,... | collective-permute-start | bytes 1572872 | tf_op jit(solution)/shard_map/ppermute | solution.py:21
  421.4 60.9 %collective-permute-start.15 = (bf16[512,512]{1,0:T(8,128)(2,1)}, bf16[512,512]{1,0:T(8,128)(2,1)}, u32[]{:S(2)}, u32[]{:S(2)}) collective-permute-start(bf16[512,512]{1,0:T(8,128)(2,1)} %get-tuple-element.25), channel_id=1, source_target_pairs={{0,254},{1,255},{2,0},{3,1},{4,2},{5,3},{6,4},{7,5},{8,6},{9,7},{1... | collective-permute-start | bytes 1572872 | tf_op jit(solution)/shard_map/ppermute | solution.py:21
  464.1 56.2 %collective-permute-start.8 = (bf16[2,512,512]{2,1,0:T(8,128)(2,1)}, bf16[2,512,512]{2,1,0:T(8,128)(2,1)S(1)}, u32[]{:S(2)}, u32[]{:S(2)}) collective-permute-start(bf16[2,512,512]{2,1,0:T(8,128)(2,1)} %get-tuple-element.21), channel_id=1, source_target_pairs={{0,128},{1,129},{2,130},{3,131},{4,132},{5,133},{6,134},{7,135},{8... | collective-permute-start | bytes 3145736 | tf_op jit(solution)/shard_map/ppermute | solution.py:21
  464.1 12.3 %copy-start.3 = (bf16[512,512]{1,0:T(8,128)(2,1)S(1)}, bf16[512,512]{1,0:T(8,128)(2,1)}, u32[]{:S(2)}) copy-start(bf16[512,512]{1,0:T(8,128)(2,1)} %copy-done.2) | copy-start | bytes 1572868
  464.1 18.1 %copy-start.1 = (bf16[512,512]{1,0:T(8,128)(2,1)S(1)}, bf16[512,512]{1,0:T(8,128)(2,1)}, u32[]{:S(2)}) copy-start(bf16[512,512]{1,0:T(8,128)(2,1)} %copy-done) | copy-start | bytes 1572868
  464.1 19.5 %copy-start.6 = (s32[6]{0:T(128)S(1)}, s32[6]{0:T(128)}, u32[]{:S(2)}) copy-start(s32[6]{0:T(128)} %constant.70.clone) | copy-start | bytes 76
  464.2 19.5 %copy-start.7 = (s32[6]{0:T(128)S(1)}, s32[6]{0:T(128)}, u32[]{:S(2)}) copy-start(s32[6]{0:T(128)} %constant.71.clone) | copy-start | bytes 76
  473.4 46.9 %collective-permute-start.12 = (bf16[1,512,512]{2,1,0:T(8,128)(2,1)S(1)}, bf16[1,512,512]{2,1,0:T(8,128)(2,1)S(1)}, u32[]{:S(2)}, u32[]{:S(2)}) collective-permute-start(bf16[1,512,512]{2,1,0:T(8,128)(2,1)S(1)} %get-tuple-element.22), channel_id=1, source_target_pairs={{0,128},{1,129},{2,130},{3,131},{4,132},{5,133},{6,134},{7,135},{8... | collective-permute-start | bytes 1572872 | tf_op jit(solution)/shard_map/ppermute | solution.py:21
  476.4 43.8 %collective-permute-start.16 = (bf16[512,512]{1,0:T(8,128)(2,1)S(1)}, bf16[512,512]{1,0:T(8,128)(2,1)S(1)}, u32[]{:S(2)}, u32[]{:S(2)}) collective-permute-start(bf16[512,512]{1,0:T(8,128)(2,1)S(1)} %copy-done.3), channel_id=1, source_target_pairs={{0,3},{1,2},{2,5},{3,4},{4,7},{5,6},{6,9},{7,8},{8,11},{9,10},{10,... | collective-permute-start | bytes 1572872 | tf_op jit(solution)/shard_map/ppermute | solution.py:21
  482.2 38.0 %collective-permute-start.17 = (bf16[512,512]{1,0:T(8,128)(2,1)S(1)}, bf16[512,512]{1,0:T(8,128)(2,1)S(1)}, u32[]{:S(2)}, u32[]{:S(2)}) collective-permute-start(bf16[512,512]{1,0:T(8,128)(2,1)S(1)} %copy-done.1), channel_id=1, source_target_pairs={{0,255},{1,254},{2,1},{3,0},{4,3},{5,2},{6,5},{7,4},{8,7},{9,6},{1... | collective-permute-start | bytes 1572872 | tf_op jit(solution)/shard_map/ppermute | solution.py:21
  483.6 36.7 %collective-permute-start.18 = (bf16[512,512]{1,0:T(8,128)(2,1)S(1)}, bf16[512,512]{1,0:T(8,128)(2,1)S(1)}, u32[]{:S(2)}, u32[]{:S(2)}) collective-permute-start(bf16[512,512]{1,0:T(8,128)(2,1)S(1)} %get-tuple-element.28), channel_id=1, source_target_pairs={{0,253},{1,4},{2,255},{3,6},{4,1},{5,8},{6,3},{7,10},{8,5},{9,12},... | collective-permute-start | bytes 1572872 | tf_op jit(solution)/shard_map/ppermute | solution.py:21
  (3 other events, 3.7 us)

commit v2 on v1

v2 whole, which is shorter than its diff:
```python
import jax
import jax.numpy as jnp
from jax import lax
from jax.experimental import pallas as pl
from jax.experimental.pallas import tpu as pltpu
from jax.sharding import PartitionSpec as P

N = 256
SEAM = 128
SEAM_AT = 32
PLANE = 64
B = 512
HALF = 4096
TAG = 128
WIDE = HALF + TAG
NSTEP = 256
ROWS = 64
MIB = 1024 * 1024


def send(block, target, only=None):
    pairs = [(i, target(i) % N) for i in range(N) if only is None or only(i)]
    return lax.ppermute(block, "blk", pairs)


def hold(block, *others):
    return lax.optimization_barrier((block,) + others)[0]


def at(y, z, x, core):
    return ((y % 4 * 8 + z % 8) * 4 + x % 4) * 2 + core


def corner(i):
    spot = i % PLANE
    side = 1 if spot < 2 else 2 if spot >= PLANE - 2 else 0
    return i // PLANE, side, i % 2


DOWN = {(0, 0): (0, 0), (0, 1): (7, 0)}
UP = {(0, 0): (7, 3), (0, 1): (0, 3)}
SPLIT = 336


def border_routes(part):
    first, second = [], []
    for y in range(4):
        for core in range(2):
            for source, plane, via, goal in (
                (at(y, 0, 0, core), y - 1, DOWN, at(y - 1, 7, 3, core)),
                (at(y, 7, 3, core), y + 1, UP, at(y + 1, 0, 0, core)),
            ):
                if (part, core) in via:
                    middle = at(plane, *via[part, core], core)
                    first.append((source, middle))
                    second.append((middle, goal))
                else:
                    first.append((source, goal))
    return first, second


def unit_kernel(info, x_ref, tag_ref, keep_ref, other_ref, ahead_ref):
    x = x_ref[...].astype(jnp.float32)
    squares = jnp.sum(x * x, axis=1, keepdims=True)
    unit = (x * (1.0 / jnp.sqrt(squares + 1e-06))).astype(jnp.bfloat16)
    low, high = unit[:, :HALF], unit[:, HALF:]
    tag = tag_ref[...]

    def put(ref, half):
        @pl.when(half == 0)
        def _():
            ref[:, :HALF] = low

        @pl.when(half != 0)
        def _():
            ref[:, :HALF] = high

        ref[:, HALF:] = tag

    put(keep_ref, info[0])
    put(other_ref, 1 - info[0])
    put(ahead_ref, info[1])


def make_units(features, tags, own_half, ahead_half):
    out = jax.ShapeDtypeStruct((B, WIDE), jnp.bfloat16)
    spec = pl.BlockSpec((ROWS, WIDE), lambda r, info: (r, 0))
    return pl.pallas_call(
        unit_kernel,
        out_shape=(out, out, out),
        grid_spec=pltpu.PrefetchScalarGridSpec(
            num_scalar_prefetch=1,
            grid=(B // ROWS,),
            in_specs=[
                pl.BlockSpec((ROWS, 2 * HALF), lambda r, info: (r, 0)),
                pl.BlockSpec((ROWS, TAG), lambda r, info: (r, 0)),
            ],
            out_specs=(spec, spec, spec),
        ),
        compiler_params=pltpu.CompilerParams(vmem_limit_bytes=40 * MIB),
        cost_estimate=pl.CostEstimate(flops=12 * B * HALF, bytes_accessed=20 * MIB, transcendentals=B),
        name="units",
    )(jnp.stack([own_half, ahead_half]).astype(jnp.int32), features, tags)


def tiles(rows, blocks, row_choice, block_choice, seam_tiles, stacked=(), extra=None):
    count = len(blocks)
    used_rows = len(rows)
    flat = [array for entry in blocks for array in entry]
    alone = [t for t in range(count) if t not in stacked]
    lead = 0 if extra is None else 1

    def kernel(info, *refs):
        row_refs = refs[:used_rows]
        block_refs = []
        at_ref = used_rows
        for entry in blocks:
            block_refs.append(refs[at_ref : at_ref + len(entry)])
            at_ref += len(entry)
        if lead:
            extra_ref = refs[at_ref]
            at_ref += 1
        out_ref = refs[at_ref]
        turned = {t: refs[at_ref + 1 + k] for k, t in enumerate(alone)}
        at_ref += 1 + len(alone)
        if stacked:
            for k, t in enumerate(stacked):
                turned[t] = refs[at_ref].at[lead + k]
            stack_ref = refs[at_ref]
            at_ref += 1
        held_rows, held_blocks, row_sems, block_sems = refs[at_ref:]

        pltpu.make_async_copy(row_refs[0], held_rows.at[0], row_sems.at[0]).start()
        for t in range(count):
            for c, ref in enumerate(block_refs[t]):
                @pl.when(info[1 + t] == c)
                def _(t=t, ref=ref):
                    pltpu.make_async_copy(ref, held_blocks.at[t], block_sems.at[t]).start()
            if t == 0:
                for c in range(1, used_rows):
                    @pl.when(info[0] == c)
                    def _(c=c):
                        pltpu.make_async_copy(row_refs[c], held_rows.at[1], row_sems.at[1]).start()

        pltpu.make_async_copy(row_refs[0], held_rows.at[0], row_sems.at[0]).wait()
        if lead:
            stack_ref[0] = extra_ref[...]
        waited = False
        for t in range(count):
            which = 0
            if t in seam_tiles:
                if not waited:
                    @pl.when(info[0] > 0)
                    def _():
                        pltpu.make_async_copy(row_refs[0], held_rows.at[1], row_sems.at[1]).wait()
                    waited = True
                which = jnp.minimum(info[0], 1)
            pltpu.make_async_copy(block_refs[t][0], held_blocks.at[t], block_sems.at[t]).wait()

            def chunk(n, _, t=t, which=which):
                span = pl.ds(pl.multiple_of(n * NSTEP, NSTEP), NSTEP)
                over = (((1,), (1,)), ((), ()))
                tile = lax.dot_general(
                    held_rows[which, :, :HALF], held_blocks[t, span, :HALF], over, preferred_element_type=jnp.float32
                )
                same = lax.dot_general(
                    held_rows[which, :, HALF:], held_blocks[t, span, HALF:], over, preferred_element_type=jnp.float32
                )
                tile = jnp.where(same > 0.5, jnp.float32(0.0), tile)
                out_ref[t, :, span] = tile.astype(jnp.bfloat16)
                turned[t][span, :] = tile.T.astype(jnp.bfloat16)
                return 0

            lax.fori_loop(0, B // NSTEP, chunk, 0)

    one = jax.ShapeDtypeStruct((B, B), jnp.bfloat16)
    whole = pl.BlockSpec(memory_space=pltpu.VMEM)
    info = jnp.stack([row_choice] + list(block_choice)).astype(jnp.int32)
    outs = (jax.ShapeDtypeStruct((count, B, B), jnp.bfloat16),) + (one,) * len(alone)
    if stacked:
        outs += (jax.ShapeDtypeStruct((lead + len(stacked), B, B), jnp.bfloat16),)
    return pl.pallas_call(
        kernel,
        out_shape=outs,
        in_specs=[pl.BlockSpec(memory_space=pltpu.SMEM)]
        + [pl.BlockSpec(memory_space=pl.ANY)] * (used_rows + len(flat))
        + [whole] * lead,
        out_specs=(whole,) * len(outs),
        scratch_shapes=[
            pltpu.VMEM((2, B, WIDE), jnp.bfloat16),
            pltpu.VMEM((count, B, WIDE), jnp.bfloat16),
            pltpu.SemaphoreType.DMA((2,)),
            pltpu.SemaphoreType.DMA((count,)),
        ],
        compiler_params=pltpu.CompilerParams(vmem_limit_bytes=50 * MIB),
        cost_estimate=pl.CostEstimate(
            flops=2 * count * B * B * HALF, bytes_accessed=4 * MIB * (1 + count), transcendentals=0
        ),
        name="tiles",
    )(info, *rows, *flat, *([extra] if lead else []))


def merge_kernel(info, low, high, after_in, before_in, after, before, held_low, held_high, sems):
    def fill(ref):
        into = [
            pltpu.make_async_copy(low, held_low, sems.at[0]),
            pltpu.make_async_copy(high, held_high, sems.at[1]),
        ]
        out = [
            pltpu.make_async_copy(held_low, ref.at[pl.ds(0, SPLIT)], sems.at[2]),
            pltpu.make_async_copy(held_high, ref.at[pl.ds(SPLIT, B - SPLIT)], sems.at[3]),
        ]
        for copy in into:
            copy.start()
        for k in range(2):
            into[k].wait()
            out[k].start()
        for copy in out:
            copy.wait()

    for side, ref in ((2, after), (1, before)):
        @pl.when(info[0] == side)
        def _(ref=ref):
            fill(ref)


def merge(side, low, high, after, before):
    whole = pl.BlockSpec(memory_space=pl.ANY)
    out = jax.ShapeDtypeStruct((B, WIDE), jnp.bfloat16)
    return pl.pallas_call(
        merge_kernel,
        out_shape=(out, out),
        in_specs=[pl.BlockSpec(memory_space=pltpu.SMEM)] + [whole] * 4,
        out_specs=(whole, whole),
        scratch_shapes=[
            pltpu.VMEM((SPLIT, WIDE), jnp.bfloat16),
            pltpu.VMEM((B - SPLIT, WIDE), jnp.bfloat16),
            pltpu.SemaphoreType.DMA((4,)),
        ],
        input_output_aliases={3: 0, 4: 1},
        compiler_params=pltpu.CompilerParams(vmem_limit_bytes=16 * MIB),
        cost_estimate=pl.CostEstimate(flops=0, bytes_accessed=MIB, transcendentals=0),
        name="merge",
    )(side.astype(jnp.int32).reshape(1), low, high, after, before)


def sum_kernel(slots, near, mid, far, crossed, up, down, far_turned, out_ref):
    pairs = (
        (near[0], crossed[0]),
        (near[1], down[0]),
        (mid[0], up[0]),
        (mid[1], down[1]),
        (mid[2], up[1]),
        (far[0], far_turned[...]),
    )
    for k, (one, two) in enumerate(pairs):
        out_ref[slots[k]] = (one.astype(jnp.float32) + two.astype(jnp.float32)).astype(jnp.bfloat16)


def add_up(slots, *parts):
    whole = pl.BlockSpec(memory_space=pltpu.VMEM)
    return pl.pallas_call(
        sum_kernel,
        out_shape=jax.ShapeDtypeStruct((6, B, B), jnp.bfloat16),
        in_specs=[pl.BlockSpec(memory_space=pltpu.SMEM)] + [whole] * len(parts),
        out_specs=whole,
        compiler_params=pltpu.CompilerParams(vmem_limit_bytes=40 * MIB),
        cost_estimate=pl.CostEstimate(flops=6 * B * B, bytes_accessed=9 * MIB, transcendentals=0),
        name="add_up",
    )(slots, *parts)


def local(features, sources):
    me = lax.axis_index("blk")
    odd = me % 2
    place = (me - SEAM_AT) % SEAM
    spot = me % PLANE
    side = jnp.where(spot < 2, 1, jnp.where(spot >= PLANE - 2, 2, 0))
    own_half = ((me - SEAM_AT) % N) // SEAM
    tags = (sources[:, None] == jnp.arange(TAG, dtype=sources.dtype)[None, :]).astype(jnp.bfloat16)
    keep, other, ahead = make_units(features, tags, own_half, ((me - 2 - SEAM_AT) % N) // SEAM)

    def place_of(i):
        return (i - SEAM_AT) % SEAM

    after2 = send(ahead, lambda i: i - 2, lambda i: corner(i)[1] != 1)
    before2 = send(keep, lambda i: i + 2, lambda i: corner(i)[1] != 2)
    first, second = border_routes(0)
    low = lax.ppermute(lax.slice_in_dim(keep, 0, SPLIT), "blk", first)
    high = lax.ppermute(lax.slice_in_dim(keep, SPLIT, B), "blk", border_routes(1)[0])
    second_half = send(
        keep,
        lambda i: i - PLANE if place_of(i) == 1 else i + SEAM,
        lambda i: place_of(i) < 3,
    )
    opposite = send(hold(other, low, second_half), lambda i: i + SEAM)
    low = lax.ppermute(low, "blk", second)
    second_round = send(second_half, lambda i: i - PLANE, lambda i: place_of(i + PLANE) == 1)
    edge = send(
        hold(keep, low),
        lambda i: i + PLANE if i % 2 else i - PLANE,
        lambda i: i % PLANE in (2, PLANE - 3),
    )
    edge = send(edge, lambda i: i + 3 - PLANE if i % 2 else i - 3 + PLANE, lambda i: i % PLANE in (2, PLANE - 3))
    mate = send(hold(keep, after2, before2, opposite, low, high), lambda i: i ^ 1)

    after2, before2, mate = lax.optimization_barrier((after2, before2, mate))
    after2, before2 = merge(side, low, high, after2, before2)
    before3 = send(before2, lambda i: i + 1, lambda i: i % 2 == 1 and i % PLANE != PLANE - 1)
    after3 = send(after2, lambda i: i - 1, lambda i: i % 2 == 0 and i % PLANE != 0 and place_of(i) != 0)
    after_mate = send(after2, lambda i: i ^ 1)
    before_mate = send(before2, lambda i: i ^ 1)
    lone = send(hold(other, before_mate, after_mate), lambda i: i - 3, lambda i: place_of(i) == 2)

    zero = jnp.zeros((), jnp.int32)
    seam = jnp.where(place == 0, 1, jnp.where(place == 1, 2, 0))
    near, turned0, turned1 = tiles([opposite], [[mate], [after2]], zero, [zero] * 2, ())
    mid, turned2, crossed = tiles(
        [opposite, second_half, second_round],
        [[before2], [after_mate], [before_mate]],
        seam,
        [zero] * 3,
        (0, 2),
        (1, 2),
        turned0,
    )
    far_choice = jnp.where(odd == 1, jnp.where(place == SEAM - 1, 2, 1), 0)
    far_choice = jnp.where((spot == 0) | (spot == PLANE - 1), 3, far_choice)
    far, far_turned = tiles(
        [opposite, second_half],
        [[before3, after3, lone, edge]],
        jnp.where((odd == 0) & (place < 3), 1, 0),
        [far_choice],
        (0,),
    )

    near, mid, far = (send(t, lambda i: i + SEAM) for t in (near, mid, far))
    crossed = send(crossed, lambda i: i ^ 1)
    turned1, turned2, crossed = hold(turned1, before3, after3), hold(turned2, before3, after3), crossed
    up = send(jnp.stack([turned1, crossed[1]]), lambda i: i + 2)
    down = send(jnp.stack([turned2, crossed[2]]), lambda i: i - 2)
    far_turned = send(far_turned, lambda i: i + 3 if i % 2 else i - 3)
    slots = jnp.where(odd == 1, jnp.array([4, 3, 2, 5, 0, 1], jnp.int32), jnp.array([5, 3, 2, 1, 4, 0], jnp.int32))
    return jnp.transpose(add_up(slots, near, mid, far, crossed, up, down, far_turned), (1, 0, 2))


def solution(mesh):
    return jax.shard_map(
        local,
        mesh=mesh,
        in_specs=(P("blk", None), P("blk")),
        out_specs=P("blk", None, None),
        check_vma=False,
    )
```

time: 524 us -> 357 us (0.68)
  waiting for transfers between devices: 390 us -> 241 us
  starting transfers between devices: 78.2 us -> 56.1 us
    ppermute x19 -> x20, waiting for transfers between devices: 390 us -> 143 us  [send(): return lax.ppermute(block, 'blk', pairs)]
    ppermute x0 -> x3, waiting for transfers between devices: none -> 97.2 us  [the longest x1 38 us: local(): lax.ppermute(lax.slice_in_dim(keep, SPLIT, B), 'blk', border_routes(1)[0])]
    ppermute x19 -> x20, starting transfers between devices: 78.2 us -> 39.7 us  [send(): return lax.ppermute(block, 'blk', pairs)]
    ppermute x0 -> x3, starting transfers between devices: none -> 16.3 us  [the longest x1 10.9 us: local(): low = lax.ppermute(lax.slice_in_dim(keep, 0, SPLIT), 'blk', first)]
    pallas_call x3 -> x4, Pallas kernels: 37.2 us -> 34.8 us  [the longest x3 32 us: tiles(): pl.pallas_call(kernel, out_shape=outs, in_specs=[pl.BlockSpec(memory_spac...]
  transfers between devices with their start and end apart: 19 -> 23, of which waited for: 4 -> 11; matrix products, arithmetic and copies ran while one was open for 0% -> 2% of each run, Pallas kernels for 7% -> 10%
where the time goes in v2:
time: 357 us
  waiting for transfers between devices  241 us (68%)
  starting transfers between devices  56.1 us (16%)
  Pallas kernels  50.5 us (14%)
  local copies, waits for them, and re-layouts  6.04 us (2%)
    ppermute x20, waiting for transfers between devices, send(): return lax.ppermute(block, 'blk', pairs)  143 us
    ppermute x20, starting transfers between devices, send(): return lax.ppermute(block, 'blk', pairs)  39.7 us
    ppermute x1, waiting for transfers between devices, local(): lax.ppermute(lax.slice_in_dim(keep, SPLIT, B), 'blk', border_routes(1)[0])  38 us
    ppermute x1, waiting for transfers between devices, local(): low = lax.ppermute(low, 'blk', second)  33 us
    pallas_call x3, Pallas kernels, tiles(): pl.pallas_call(kernel, out_shape=outs, in_specs=[pl.BlockSpec(memory_spac...  32 us
    ppermute x1, waiting for transfers between devices, local(): low = lax.ppermute(lax.slice_in_dim(keep, 0, SPLIT), 'blk', first)  26.1 us
    pallas_call x1, Pallas kernels, make_units(): pl.pallas_call(unit_kernel, out_shape=(out, out, out), grid_spec=pltpu.Pr...  11.5 us
    ppermute x1, starting transfers between devices, local(): low = lax.ppermute(lax.slice_in_dim(keep, 0, SPLIT), 'blk', first)  10.9 us
  transfers between devices with their start and end apart: 23, of which 11 were waited for; matrix products, arithmetic and copies ran while one was open for 2% of the time, Pallas kernels for 10%

profile of v2, /device:TPU:1, one launch (start us, length us, event | category | flops | bytes accessed | tf_op | source)
XLA Modules:
  0.0 356.5 jit_solution(8101456366175401816)
XLA Ops:
  0.9 11.5 %units.1 = (bf16[512,4224]{1,0:T(8,128)(2,1)}, bf16[512,4224]{1,0:T(8,128)(2,1)}, bf16[512,4224]{1,0:T(8,128)(2,1)S(1)}) custom-call(s32[2]{0:T(128)S(1)} %pad_add_fusion.info, bf16[512,8192]{1,0:T(8,128)(2,1)} %x_ref.1, bf16[512,128]{1,0:T(8,128)(2,1)S(1)} %fusion.tag_ref), custom_call_target="tpu_custom_call" | custom-call | flops 25165824 | bytes 20971520 | tf_op jit(solution)/shard_map/units/pallas_call | solution.py:88
  12.4 2.7 collective-permute-start.1
  17.1 10.9 %collective-permute-start = (bf16[336,4224]{1,0:T(8,128)(2,1)S(1)}, bf16[336,4224]{1,0:T(8,128)(2,1)S(1)}, u32[]{:S(2)}, u32[]{:S(2)}) collective-permute-start(bf16[336,4224]{1,0:T(8,128)(2,1)S(1)} %slice.12), channel_id=1, source_target_pairs={{0,192},{62,126},{1,249},{63,71},{64,0},{126,190},{65,57},{127,135... | collective-permute-start | bytes 8515592 | tf_op jit(solution)/shard_map/ppermute | solution.py:289
  28.1 3.3 collective-permute-start.4
  32.7 26.1 %collective-permute-done = bf16[336,4224]{1,0:T(8,128)(2,1)S(1)} collective-permute-done((bf16[336,4224]{1,0:T(8,128)(2,1)S(1)}, bf16[336,4224]{1,0:T(8,128)(2,1)S(1)}, u32[]{:S(2)}, u32[]{:S(2)}) %collective-permute-start) | collective-permute-done | bytes 2838560 | tf_op jit(solution)/shard_map/ppermute | solution.py:289
  62.0 4.1 %collective-permute-start.6 = (bf16[176,4224]{1,0:T(8,128)(2,1)S(1)}, bf16[176,4224]{1,0:T(8,128)(2,1)S(1)}, u32[]{:S(2)}, u32[]{:S(2)}) collective-permute-start(bf16[176,4224]{1,0:T(8,128)(2,1)S(1)} %slice.13), channel_id=1, source_target_pairs={{0,254},{62,64},{1,255},{63,65},{64,62},{126,128},{65,63},{127,129... | collective-permute-start | bytes 4460552 | tf_op jit(solution)/shard_map/ppermute | solution.py:290
  66.1 38.0 %collective-permute-done.6.high = bf16[176,4224]{1,0:T(8,128)(2,1)S(1)} collective-permute-done((bf16[176,4224]{1,0:T(8,128)(2,1)S(1)}, bf16[176,4224]{1,0:T(8,128)(2,1)S(1)}, u32[]{:S(2)}, u32[]{:S(2)}) %collective-permute-start.6) | collective-permute-done | bytes 1486880 | tf_op jit(solution)/shard_map/ppermute | solution.py:290
  105.2 19.5 %collective-permute-done.3.after_in = bf16[512,4224]{1,0:T(8,128)(2,1)} collective-permute-done((bf16[512,4224]{1,0:T(8,128)(2,1)S(1)}, bf16[512,4224]{1,0:T(8,128)(2,1)}, u32[]{:S(2)}, u32[]{:S(2)}) %collective-permute-start.3) | collective-permute-done | bytes 4325408 | tf_op jit(solution)/shard_map/ppermute | solution.py:23
  124.8 33.0 %collective-permute-done.5.low = bf16[336,4224]{1,0:T(8,128)(2,1)S(1)} collective-permute-done((bf16[336,4224]{1,0:T(8,128)(2,1)S(1)}, bf16[336,4224]{1,0:T(8,128)(2,1)S(1)}, u32[]{:S(2)}, u32[]{:S(2)}) %collective-permute-start.5) | collective-permute-done | bytes 2838560 | tf_op jit(solution)/shard_map/ppermute | solution.py:297
  157.8 28.1 %collective-permute-done.2.refs_0_ = bf16[512,4224]{1,0:T(8,128)(2,1)} collective-permute-done((bf16[512,4224]{1,0:T(8,128)(2,1)}, bf16[512,4224]{1,0:T(8,128)(2,1)}, u32[]{:S(2)}, u32[]{:S(2)}) %collective-permute-start.2) | collective-permute-done | bytes 4325408 | tf_op jit(solution)/shard_map/ppermute | solution.py:23
  188.5 5.1 %collective-permute-done.7.refs_1_ = bf16[512,4224]{1,0:T(8,128)(2,1)} collective-permute-done((bf16[512,4224]{1,0:T(8,128)(2,1)}, bf16[512,4224]{1,0:T(8,128)(2,1)}, u32[]{:S(2)}, u32[]{:S(2)}) %collective-permute-start.7) | collective-permute-done | bytes 4325408 | tf_op jit(solution)/shard_map/ppermute | solution.py:23
  195.0 2.8 merge.1
  198.4 2.7 collective-permute-start.9
  202.4 8.3 %collective-permute-start.13 = (bf16[512,4224]{1,0:T(8,128)(2,1)}, bf16[512,4224]{1,0:T(8,128)(2,1)}, u32[]{:S(2)}, u32[]{:S(2)}) collective-permute-start(bf16[512,4224]{1,0:T(8,128)(2,1)} %get-tuple-element.37.refs_3_), channel_id=1, source_target_pairs={{1,2},{3,4},{5,6},{7,8},{9,10},{11,12},{13,14},{15,16},{17,18},{19... | collective-permute-start | bytes 12976136 | tf_op jit(solution)/shard_map/ppermute | solution.py:23
  213.4 2.8 collective-permute-start.15
  216.3 10.7 %tiles.3 = (bf16[2,512,512]{2,1,0:T(8,128)(2,1)}, bf16[512,512]{1,0:T(8,128)(2,1)S(1)}, bf16[512,512]{1,0:T(8,128)(2,1)S(1)}) custom-call(s32[3]{0:T(128)S(1)} %broadcast_3_info.2.info, bf16[512,4224]{1,0:T(8,128)(2,1)} %collective-permute-done.2.refs_0_, bf16[512,4224]{1,0:T(8,128)(2,1)} %collective-permute-done.7.refs_1_, ...), custom_call_target="tpu_custom_call" | custom-call | flops 4294967296 | bytes 12582912 | tf_op jit(solution)/shard_map/tiles/pallas_call | solution.py:182
  227.0 14.3 %tiles.4 = (bf16[3,512,512]{2,1,0:T(8,128)(2,1)}, bf16[512,512]{1,0:T(8,128)(2,1)S(1)}, bf16[3,512,512]{2,1,0:T(8,128)(2,1)}) custom-call(s32[4]{0:T(128)S(1)} %pad_add_fusion.1.info, bf16[512,4224]{1,0:T(8,128)(2,1)} %collective-permute-done.2.refs_0_, bf16[512,4224]{1,0:T(8,128)(2,1)} %collective-permute-done.1.refs_1_, ...), custom_call_target="tpu_custom_call" | custom-call | flops 6442450944 | bytes 16777216 | tf_op jit(solution)/shard_map/tiles/pallas_call | solution.py:182
  241.4 11.5 %collective-permute-done.14.refs_3_ = bf16[512,4224]{1,0:T(8,128)(2,1)} collective-permute-done((bf16[512,4224]{1,0:T(8,128)(2,1)}, bf16[512,4224]{1,0:T(8,128)(2,1)}, u32[]{:S(2)}, u32[]{:S(2)}) %collective-permute-start.14) | collective-permute-done | bytes 4325408 | tf_op jit(solution)/shard_map/ppermute | solution.py:23
  259.3 6.9 %collective-permute-start.21 = (bf16[2,512,512]{2,1,0:T(8,128)(2,1)}, bf16[2,512,512]{2,1,0:T(8,128)(2,1)}, u32[]{:S(2)}, u32[]{:S(2)}) collective-permute-start(bf16[2,512,512]{2,1,0:T(8,128)(2,1)} %pad_maximum_fusion.1), channel_id=1, source_target_pairs={{0,254},{1,255},{2,0},{3,1},{4,2},{5,3},{6,4},{7,5},{8,6},{9,7},{1... | collective-permute-start | bytes 3145736 | tf_op jit(solution)/shard_map/ppermute | solution.py:23
  266.2 7.0 %tiles.5 = (bf16[1,512,512]{2,1,0:T(8,128)(2,1)S(1)}, bf16[512,512]{1,0:T(8,128)(2,1)S(1)}) custom-call(s32[2]{0:T(128)S(1)} %pad_add_fusion.2.info, bf16[512,4224]{1,0:T(8,128)(2,1)} %collective-permute-done.2.refs_0_, bf16[512,4224]{1,0:T(8,128)(2,1)} %collective-permute-done.1.refs_1_, bf16[512,4224]{1,0:T(8,128)(2,1)} %collective-permute-done.13.refs_2_, ...), custom_call_target="tpu_custom_call" | custom-call | flops 2147483648 | bytes 8388608 | tf_op jit(solution)/shard_map/tiles/pallas_call | solution.py:182
  274.8 38.1 %collective-permute-done.8.near = bf16[2,512,512]{2,1,0:T(8,128)(2,1)} collective-permute-done((bf16[2,512,512]{2,1,0:T(8,128)(2,1)}, bf16[2,512,512]{2,1,0:T(8,128)(2,1)}, u32[]{:S(2)}, u32[]{:S(2)}) %collective-permute-start.8) | collective-permute-done | bytes 1048608 | tf_op jit(solution)/shard_map/ppermute | solution.py:23
  312.9 33.7 %collective-permute-done.12.mid = bf16[3,512,512]{2,1,0:T(8,128)(2,1)S(1)} collective-permute-done((bf16[3,512,512]{2,1,0:T(8,128)(2,1)}, bf16[3,512,512]{2,1,0:T(8,128)(2,1)S(1)}, u32[]{:S(2)}, u32[]{:S(2)}) %collective-permute-start.12) | collective-permute-done | bytes 1572896 | tf_op jit(solution)/shard_map/ppermute | solution.py:23
  346.6 5.7 %collective-permute-done.18.far = bf16[1,512,512]{2,1,0:T(8,128)(2,1)S(1)} collective-permute-done((bf16[1,512,512]{2,1,0:T(8,128)(2,1)S(1)}, bf16[1,512,512]{2,1,0:T(8,128)(2,1)S(1)}, u32[]{:S(2)}, u32[]{:S(2)}) %collective-permute-start.18) | collective-permute-done | bytes 524320 | tf_op jit(solution)/shard_map/ppermute | solution.py:23
  352.3 4.2 %add_up.1 = bf16[6,512,512]{2,1,0:T(8,128)(2,1)} custom-call(s32[6]{0:T(128)S(1)} %broadcast_select_fusion.slots, bf16[2,512,512]{2,1,0:T(8,128)(2,1)} %collective-permute-done.8.near, bf16[3,512,512]{2,1,0:T(8,128)(2,1)S(1)} %collective-permute-done.12.mid, bf16[1,512,512]{2,1,0:T(8,128)(2,1)S(1)} %collective-permute-done.18.far, ...), custom_call_target="tpu_custom_call" | custom-call | flops 1572864 | bytes 9437184 | tf_op jit(solution)/shard_map/add_up/pallas_call | solution.py:262
  (48 shorter events, 25.1 us)
Async XLA Ops:
  12.4 46.4 %collective-permute-start.1 = (bf16[512,4224]{1,0:T(8,128)(2,1)}, bf16[512,4224]{1,0:T(8,128)(2,1)}, u32[]{:S(2)}, u32[]{:S(2)}) collective-permute-start(bf16[512,4224]{1,0:T(8,128)(2,1)} %get-tuple-element.41), channel_id=1, source_target_pairs={{32,160},{33,225},{34,162},{160,32},{161,97},{162,34}} | collective-permute-start | bytes 12976136 | tf_op jit(solution)/shard_map/ppermute | solution.py:23
  17.1 41.7 %collective-permute-start = (bf16[336,4224]{1,0:T(8,128)(2,1)S(1)}, bf16[336,4224]{1,0:T(8,128)(2,1)S(1)}, u32[]{:S(2)}, u32[]{:S(2)}) collective-permute-start(bf16[336,4224]{1,0:T(8,128)(2,1)S(1)} %slice.12), channel_id=1, source_target_pairs={{0,192},{62,126},{1,249},{63,71},{64,0},{126,190},{65,57},{127,135... | collective-permute-start | bytes 8515592 | tf_op jit(solution)/shard_map/ppermute | solution.py:289
  28.1 96.7 %collective-permute-start.4 = (bf16[512,4224]{1,0:T(8,128)(2,1)}, bf16[512,4224]{1,0:T(8,128)(2,1)}, u32[]{:S(2)}, u32[]{:S(2)}) collective-permute-start(bf16[512,4224]{1,0:T(8,128)(2,1)} %get-tuple-element.41), channel_id=1, source_target_pairs={{0,2},{1,3},{2,4},{3,5},{4,6},{5,7},{6,8},{7,9},{8,10},{9,11},{10,... | collective-permute-start | bytes 12976136 | tf_op jit(solution)/shard_map/ppermute | solution.py:23
  31.4 93.3 %collective-permute-start.3 = (bf16[512,4224]{1,0:T(8,128)(2,1)S(1)}, bf16[512,4224]{1,0:T(8,128)(2,1)}, u32[]{:S(2)}, u32[]{:S(2)}) collective-permute-start(bf16[512,4224]{1,0:T(8,128)(2,1)S(1)} %get-tuple-element.30), channel_id=1, source_target_pairs={{2,0},{3,1},{4,2},{5,3},{6,4},{7,5},{8,6},{9,7},{10,8},{11,9},{12,... | collective-permute-start | bytes 12976136 | tf_op jit(solution)/shard_map/ppermute | solution.py:23
  58.8 127.0 %collective-permute-start.2 = (bf16[512,4224]{1,0:T(8,128)(2,1)}, bf16[512,4224]{1,0:T(8,128)(2,1)}, u32[]{:S(2)}, u32[]{:S(2)}) collective-permute-start(bf16[512,4224]{1,0:T(8,128)(2,1)} %get-tuple-element.40), channel_id=1, source_target_pairs={{0,128},{1,129},{2,130},{3,131},{4,132},{5,133},{6,134},{7,135},{8... | collective-permute-start | bytes 12976136 | tf_op jit(solution)/shard_map/ppermute | solution.py:23
  59.2 98.6 %collective-permute-start.5 = (bf16[336,4224]{1,0:T(8,128)(2,1)S(1)}, bf16[336,4224]{1,0:T(8,128)(2,1)S(1)}, u32[]{:S(2)}, u32[]{:S(2)}) collective-permute-start(bf16[336,4224]{1,0:T(8,128)(2,1)S(1)} %collective-permute-done), channel_id=1, source_target_pairs={{192,254},{126,64},{249,255},{71,65},{0,62},{190,128},{57,63},{135... | collective-permute-start | bytes 8515592 | tf_op jit(solution)/shard_map/ppermute | solution.py:297
  62.0 42.1 %collective-permute-start.6 = (bf16[176,4224]{1,0:T(8,128)(2,1)S(1)}, bf16[176,4224]{1,0:T(8,128)(2,1)S(1)}, u32[]{:S(2)}, u32[]{:S(2)}) collective-permute-start(bf16[176,4224]{1,0:T(8,128)(2,1)S(1)} %slice.13), channel_id=1, source_target_pairs={{0,254},{62,64},{1,255},{63,65},{64,62},{126,128},{65,63},{127,129... | collective-permute-start | bytes 4460552 | tf_op jit(solution)/shard_map/ppermute | solution.py:290
  185.9 7.7 %collective-permute-start.7 = (bf16[512,4224]{1,0:T(8,128)(2,1)}, bf16[512,4224]{1,0:T(8,128)(2,1)}, u32[]{:S(2)}, u32[]{:S(2)}) collective-permute-start(bf16[512,4224]{1,0:T(8,128)(2,1)} %get-tuple-element.41), channel_id=1, source_target_pairs={{0,1},{1,0},{2,3},{3,2},{4,5},{5,4},{6,7},{7,6},{8,9},{9,8},{10,11... | collective-permute-start | bytes 12976136 | tf_op jit(solution)/shard_map/ppermute | solution.py:23
  185.9 16.5 %collective-permute-start.16 = (bf16[512,4224]{1,0:T(8,128)(2,1)}, bf16[512,4224]{1,0:T(8,128)(2,1)}, u32[]{:S(2)}, u32[]{:S(2)}) collective-permute-start(bf16[512,4224]{1,0:T(8,128)(2,1)} %get-tuple-element.41), channel_id=1, source_target_pairs={{2,194},{61,125},{66,2},{125,189},{130,66},{189,253},{194,130},{25... | collective-permute-start | bytes 12976136 | tf_op jit(solution)/shard_map/ppermute | solution.py:23
  197.8 12.9 %collective-permute-start.10 = (bf16[512,4224]{1,0:T(8,128)(2,1)}, bf16[512,4224]{1,0:T(8,128)(2,1)}, u32[]{:S(2)}, u32[]{:S(2)}) collective-permute-start(bf16[512,4224]{1,0:T(8,128)(2,1)} %get-tuple-element.35.refs_2_), channel_id=1, source_target_pairs={{0,1},{1,0},{2,3},{3,2},{4,5},{5,4},{6,7},{7,6},{8,9},{9,8},{10,11... | collective-permute-start | bytes 12976136 | tf_op jit(solution)/shard_map/ppermute | solution.py:23
  198.0 15.3 %collective-permute-start.11 = (bf16[512,4224]{1,0:T(8,128)(2,1)}, bf16[512,4224]{1,0:T(8,128)(2,1)}, u32[]{:S(2)}, u32[]{:S(2)}) collective-permute-start(bf16[512,4224]{1,0:T(8,128)(2,1)} %get-tuple-element.37.refs_3_), channel_id=1, source_target_pairs={{0,1},{1,0},{2,3},{3,2},{4,5},{5,4},{6,7},{7,6},{8,9},{9,8},{10,11... | collective-permute-start | bytes 12976136 | tf_op jit(solution)/shard_map/ppermute | solution.py:23
  198.4 28.6 %collective-permute-start.9 = (bf16[512,4224]{1,0:T(8,128)(2,1)}, bf16[512,4224]{1,0:T(8,128)(2,1)}, u32[]{:S(2)}, u32[]{:S(2)}) collective-permute-start(bf16[512,4224]{1,0:T(8,128)(2,1)} %collective-permute-done.1.refs_1_), channel_id=1, source_target_pairs={{97,33},{225,161}} | collective-permute-start | bytes 12976136 | tf_op jit(solution)/shard_map/ppermute | solution.py:23
  201.1 51.8 %collective-permute-start.14 = (bf16[512,4224]{1,0:T(8,128)(2,1)}, bf16[512,4224]{1,0:T(8,128)(2,1)}, u32[]{:S(2)}, u32[]{:S(2)}) collective-permute-start(bf16[512,4224]{1,0:T(8,128)(2,1)} %get-tuple-element.35.refs_2_), channel_id=1, source_target_pairs={{2,1},{4,3},{6,5},{8,7},{10,9},{12,11},{14,13},{16,15},{18,17},{20... | collective-permute-start | bytes 12976136 | tf_op jit(solution)/shard_map/ppermute | solution.py:23
  202.4 53.4 %collective-permute-start.13 = (bf16[512,4224]{1,0:T(8,128)(2,1)}, bf16[512,4224]{1,0:T(8,128)(2,1)}, u32[]{:S(2)}, u32[]{:S(2)}) collective-permute-start(bf16[512,4224]{1,0:T(8,128)(2,1)} %get-tuple-element.37.refs_3_), channel_id=1, source_target_pairs={{1,2},{3,4},{5,6},{7,8},{9,10},{11,12},{13,14},{15,16},{17,18},{19... | collective-permute-start | bytes 12976136 | tf_op jit(solution)/shard_map/ppermute | solution.py:23
  210.7 48.5 %collective-permute-start.17 = (bf16[512,4224]{1,0:T(8,128)(2,1)}, bf16[512,4224]{1,0:T(8,128)(2,1)}, u32[]{:S(2)}, u32[]{:S(2)}) collective-permute-start(bf16[512,4224]{1,0:T(8,128)(2,1)} %collective-permute-done.16), channel_id=1, source_target_pairs={{2,63},{61,0},{66,127},{125,64},{130,191},{189,128},{194,255},{253... | collective-permute-start | bytes 12976136 | tf_op jit(solution)/shard_map/ppermute | solution.py:23
  213.4 52.9 %collective-permute-start.15 = (bf16[512,4224]{1,0:T(8,128)(2,1)}, bf16[512,4224]{1,0:T(8,128)(2,1)}, u32[]{:S(2)}, u32[]{:S(2)}) collective-permute-start(bf16[512,4224]{1,0:T(8,128)(2,1)} %get-tuple-element.40), channel_id=1, source_target_pairs={{34,31},{162,159}} | collective-permute-start | bytes 12976136 | tf_op jit(solution)/shard_map/ppermute | solution.py:23
  241.3 15.8 %collective-permute-start.19 = (bf16[3,512,512]{2,1,0:T(8,128)(2,1)}, bf16[3,512,512]{2,1,0:T(8,128)(2,1)S(1)}, u32[]{:S(2)}, u32[]{:S(2)}) collective-permute-start(bf16[3,512,512]{2,1,0:T(8,128)(2,1)} %get-tuple-element.43), channel_id=1, source_target_pairs={{0,1},{1,0},{2,3},{3,2},{4,5},{5,4},{6,7},{7,6},{8,9},{9,8},{10,11... | collective-permute-start | bytes 4718600 | tf_op jit(solution)/shard_map/ppermute | solution.py:23
  252.9 60.0 %collective-permute-start.8 = (bf16[2,512,512]{2,1,0:T(8,128)(2,1)}, bf16[2,512,512]{2,1,0:T(8,128)(2,1)}, u32[]{:S(2)}, u32[]{:S(2)}) collective-permute-start(bf16[2,512,512]{2,1,0:T(8,128)(2,1)} %get-tuple-element.36), channel_id=1, source_target_pairs={{0,128},{1,129},{2,130},{3,131},{4,132},{5,133},{6,134},{7,135},{8... | collective-permute-start | bytes 3145736 | tf_op jit(solution)/shard_map/ppermute | solution.py:23
  255.8 90.8 %collective-permute-start.12 = (bf16[3,512,512]{2,1,0:T(8,128)(2,1)}, bf16[3,512,512]{2,1,0:T(8,128)(2,1)S(1)}, u32[]{:S(2)}, u32[]{:S(2)}) collective-permute-start(bf16[3,512,512]{2,1,0:T(8,128)(2,1)} %get-tuple-element.39), channel_id=1, source_target_pairs={{0,128},{1,129},{2,130},{3,131},{4,132},{5,133},{6,134},{7,135},{8... | collective-permute-start | bytes 4718600 | tf_op jit(solution)/shard_map/ppermute | solution.py:23
  258.2 88.4 %collective-permute-start.20 = (bf16[2,512,512]{2,1,0:T(8,128)(2,1)}, bf16[2,512,512]{2,1,0:T(8,128)(2,1)}, u32[]{:S(2)}, u32[]{:S(2)}) collective-permute-start(bf16[2,512,512]{2,1,0:T(8,128)(2,1)} %pad_maximum_fusion), channel_id=1, source_target_pairs={{0,2},{1,3},{2,4},{3,5},{4,6},{5,7},{6,8},{7,9},{8,10},{9,11},{10,... | collective-permute-start | bytes 3145736 | tf_op jit(solution)/shard_map/ppermute | solution.py:23
  259.3 87.3 %collective-permute-start.21 = (bf16[2,512,512]{2,1,0:T(8,128)(2,1)}, bf16[2,512,512]{2,1,0:T(8,128)(2,1)}, u32[]{:S(2)}, u32[]{:S(2)}) collective-permute-start(bf16[2,512,512]{2,1,0:T(8,128)(2,1)} %pad_maximum_fusion.1), channel_id=1, source_target_pairs={{0,254},{1,255},{2,0},{3,1},{4,2},{5,3},{6,4},{7,5},{8,6},{9,7},{1... | collective-permute-start | bytes 3145736 | tf_op jit(solution)/shard_map/ppermute | solution.py:23
  266.2 46.6 %copy-start.3 = (s32[6]{0:T(128)S(1)}, s32[6]{0:T(128)}, u32[]{:S(2)}) copy-start(s32[6]{0:T(128)} %constant.93.clone) | copy-start | bytes 76
  273.2 79.1 %collective-permute-start.18 = (bf16[1,512,512]{2,1,0:T(8,128)(2,1)S(1)}, bf16[1,512,512]{2,1,0:T(8,128)(2,1)S(1)}, u32[]{:S(2)}, u32[]{:S(2)}) collective-permute-start(bf16[1,512,512]{2,1,0:T(8,128)(2,1)S(1)} %get-tuple-element.42), channel_id=1, source_target_pairs={{0,128},{1,129},{2,130},{3,131},{4,132},{5,133},{6,134},{7,135},{8... | collective-permute-start | bytes 1572872 | tf_op jit(solution)/shard_map/ppermute | solution.py:23
  312.9 39.4 %collective-permute-start.22 = (bf16[512,512]{1,0:T(8,128)(2,1)S(1)}, bf16[512,512]{1,0:T(8,128)(2,1)S(1)}, u32[]{:S(2)}, u32[]{:S(2)}) collective-permute-start(bf16[512,512]{1,0:T(8,128)(2,1)S(1)} %get-tuple-element.48), channel_id=1, source_target_pairs={{0,253},{1,4},{2,255},{3,6},{4,1},{5,8},{6,3},{7,10},{8,5},{9,12},... | collective-permute-start | bytes 1572872 | tf_op jit(solution)/shard_map/ppermute | solution.py:23
  (3 other events, 49.1 us)

commit v3 on v2

v3 whole, which is shorter than its diff:
```python
import jax
import jax.numpy as jnp
from jax import lax
from jax.experimental import pallas as pl
from jax.experimental.pallas import tpu as pltpu
from jax.sharding import PartitionSpec as P

N = 256
SEAM = 128
SEAM_AT = 32
PLANE = 64
B = 512
HALF = 4096
TAG = 128
WIDE = HALF + TAG
NSTEP = 256
ROWS = 64
MIB = 1024 * 1024


def send(block, target, only=None):
    pairs = [(i, target(i) % N) for i in range(N) if only is None or only(i)]
    return lax.ppermute(block, "blk", pairs)


def hold(block, *others):
    return lax.optimization_barrier((block,) + others)[0]


def at(y, z, x, core):
    return ((y % 4 * 8 + z % 8) * 4 + x % 4) * 2 + core


def border_side(i):
    spot = i % PLANE
    return 1 if spot < 2 else 2 if spot >= PLANE - 2 else 0


def border_routes():
    first, second = [], []
    for y in range(4):
        first += [
            (at(y, 0, 0, 1), at(y - 1, 7, 3, 1)),
            (at(y, 7, 3, 1), at(y + 1, 0, 0, 1)),
            (at(y, 0, 0, 0), at(y - 1, 0, 0, 0)),
            (at(y, 7, 3, 0), at(y + 1, 7, 3, 0)),
            (at(y, 7, 2, 1), at(y + 1, 7, 2, 1)),
            (at(y, 0, 1, 0), at(y - 1, 0, 1, 0)),
        ]
        second += [(at(y, 0, 0, 0), at(y, 7, 3, 0)), (at(y, 7, 3, 0), at(y, 0, 0, 0))]
    return first, second


def edge_routes():
    border = [pair for y in range(4) for pair in ((at(y, 7, 2, 1), at(y, 0, 0, 0)), (at(y, 0, 1, 0), at(y, 7, 3, 1)))]
    return border + [(i, (i - 3) % N) for i in range(N) if (i - SEAM_AT) % SEAM == 2]


def unit_kernel(info, x_ref, tag_ref, keep_ref, other_ref, ahead_ref):
    x = x_ref[...].astype(jnp.float32)
    squares = jnp.sum(x * x, axis=1, keepdims=True)
    unit = (x * (1.0 / jnp.sqrt(squares + 1e-06))).astype(jnp.bfloat16)
    low, high = unit[:, :HALF], unit[:, HALF:]
    tag = tag_ref[...]

    def put(ref, half):
        @pl.when(half == 0)
        def _():
            ref[:, :HALF] = low

        @pl.when(half != 0)
        def _():
            ref[:, :HALF] = high

        ref[:, HALF:] = tag

    put(keep_ref, info[0])
    put(other_ref, 1 - info[0])
    put(ahead_ref, info[1])


def make_units(features, tags, own_half, ahead_half):
    out = jax.ShapeDtypeStruct((B, WIDE), jnp.bfloat16)
    spec = pl.BlockSpec((ROWS, WIDE), lambda r, info: (r, 0))
    return pl.pallas_call(
        unit_kernel,
        out_shape=(out, out, out),
        grid_spec=pltpu.PrefetchScalarGridSpec(
            num_scalar_prefetch=1,
            grid=(B // ROWS,),
            in_specs=[
                pl.BlockSpec((ROWS, 2 * HALF), lambda r, info: (r, 0)),
                pl.BlockSpec((ROWS, TAG), lambda r, info: (r, 0)),
            ],
            out_specs=(spec, spec, spec),
        ),
        compiler_params=pltpu.CompilerParams(vmem_limit_bytes=40 * MIB),
        cost_estimate=pl.CostEstimate(flops=12 * B * HALF, bytes_accessed=20 * MIB, transcendentals=B),
        name="units",
    )(jnp.stack([own_half, ahead_half]).astype(jnp.int32), features, tags)


def tiles(rows, blocks, row_choice, block_choice, seam_tiles, stacked=()):
    count = len(blocks)
    used_rows = len(rows)
    blocks = [[option if isinstance(option, tuple) else (option,) for option in entry] for entry in blocks]
    flat = [array for entry in blocks for option in entry for array in option]
    alone = [t for t in range(count) if t not in stacked]

    def kernel(info, *refs):
        row_refs = refs[:used_rows]
        block_refs = []
        at_ref = used_rows
        for entry in blocks:
            block_refs.append([])
            for option in entry:
                block_refs[-1].append(refs[at_ref : at_ref + len(option)])
                at_ref += len(option)
        out_ref = refs[at_ref]
        turned = {t: refs[at_ref + 1 + k] for k, t in enumerate(alone)}
        at_ref += 1 + len(alone)
        if stacked:
            for k, t in enumerate(stacked):
                turned[t] = refs[at_ref].at[k]
            at_ref += 1
        held_rows, held_blocks, row_sems, block_sems = refs[at_ref:]

        pltpu.make_async_copy(row_refs[0], held_rows.at[0], row_sems.at[0]).start()
        for t in range(count):
            for c, pieces in enumerate(block_refs[t]):
                @pl.when(info[1 + t] == c)
                def _(t=t, pieces=pieces):
                    row = 0
                    for ref in pieces:
                        into = held_blocks.at[t, pl.ds(row, ref.shape[0])]
                        pltpu.make_async_copy(ref, into, block_sems.at[t]).start()
                        row += ref.shape[0]
            if t == 0:
                for c in range(1, used_rows):
                    @pl.when(info[0] == c)
                    def _(c=c):
                        pltpu.make_async_copy(row_refs[c], held_rows.at[1], row_sems.at[1]).start()

        pltpu.make_async_copy(row_refs[0], held_rows.at[0], row_sems.at[0]).wait()
        waited = False
        for t in range(count):
            which = 0
            if t in seam_tiles:
                if not waited:
                    @pl.when(info[0] > 0)
                    def _():
                        pltpu.make_async_copy(row_refs[0], held_rows.at[1], row_sems.at[1]).wait()
                    waited = True
                which = jnp.minimum(info[0], 1)
            pltpu.make_async_copy(held_blocks.at[t], held_blocks.at[t], block_sems.at[t]).wait()

            def chunk(n, _, t=t, which=which):
                span = pl.ds(pl.multiple_of(n * NSTEP, NSTEP), NSTEP)
                over = (((1,), (1,)), ((), ()))
                tile = lax.dot_general(
                    held_rows[which, :, :HALF], held_blocks[t, span, :HALF], over, preferred_element_type=jnp.float32
                )
                same = lax.dot_general(
                    held_rows[which, :, HALF:], held_blocks[t, span, HALF:], over, preferred_element_type=jnp.float32
                )
                tile = jnp.where(same > 0.5, jnp.float32(0.0), tile)
                out_ref[t, :, span] = tile.astype(jnp.bfloat16)
                turned[t][span, :] = tile.T.astype(jnp.bfloat16)
                return 0

            lax.fori_loop(0, B // NSTEP, chunk, 0)

    one = jax.ShapeDtypeStruct((B, B), jnp.bfloat16)
    whole = pl.BlockSpec(memory_space=pltpu.VMEM)
    info = jnp.stack([row_choice] + list(block_choice)).astype(jnp.int32)
    outs = (jax.ShapeDtypeStruct((count, B, B), jnp.bfloat16),) + (one,) * len(alone)
    if stacked:
        outs += (jax.ShapeDtypeStruct((len(stacked), B, B), jnp.bfloat16),)
    return pl.pallas_call(
        kernel,
        out_shape=outs,
        in_specs=[pl.BlockSpec(memory_space=pltpu.SMEM)]
        + [pl.BlockSpec(memory_space=pl.ANY)] * (used_rows + len(flat)),
        out_specs=(whole,) * len(outs),
        scratch_shapes=[
            pltpu.VMEM((2, B, WIDE), jnp.bfloat16),
            pltpu.VMEM((count, B, WIDE), jnp.bfloat16),
            pltpu.SemaphoreType.DMA((2,)),
            pltpu.SemaphoreType.DMA((count,)),
        ],
        compiler_params=pltpu.CompilerParams(vmem_limit_bytes=50 * MIB),
        cost_estimate=pl.CostEstimate(
            flops=2 * count * B * B * HALF, bytes_accessed=4 * MIB * (1 + count), transcendentals=0
        ),
        name="tiles",
    )(info, *rows, *flat)


def merge_kernel(info, even, odd, after_in, before_in, after, before, held, sems):
    for side, ref in ((2, after), (1, before)):
        for core, source in ((0, even), (1, odd)):
            @pl.when((info[0] == side) & (info[1] == core))
            def _(ref=ref, source=source):
                for out in (False, True):
                    copies = []
                    for k in range(4):
                        rows = pl.ds(k * B // 4, B // 4)
                        pair = (held.at[rows], ref.at[rows]) if out else (source.at[rows], held.at[rows])
                        copies.append(pltpu.make_async_copy(*pair, sems.at[k]))
                    for copy in copies:
                        copy.start()
                    for copy in copies:
                        copy.wait()


def merge(side, core, even, odd, after, before):
    whole = pl.BlockSpec(memory_space=pl.ANY)
    out = jax.ShapeDtypeStruct((B, WIDE), jnp.bfloat16)
    return pl.pallas_call(
        merge_kernel,
        out_shape=(out, out),
        in_specs=[pl.BlockSpec(memory_space=pltpu.SMEM)] + [whole] * 4,
        out_specs=(whole, whole),
        scratch_shapes=[pltpu.VMEM((B, WIDE), jnp.bfloat16), pltpu.SemaphoreType.DMA((4,))],
        input_output_aliases={3: 0, 4: 1},
        compiler_params=pltpu.CompilerParams(vmem_limit_bytes=16 * MIB),
        cost_estimate=pl.CostEstimate(flops=0, bytes_accessed=MIB, transcendentals=0),
        name="merge",
    )(jnp.stack([side, core]).astype(jnp.int32), even, odd, after, before)


def sum_kernel(slots, near, far, crossed, up, down, far_turned, out_ref):
    pairs = (
        (near[2], crossed[0]),
        (near[0], down[0]),
        (near[1], up[0]),
        (near[3], down[1]),
        (near[4], up[1]),
        (far[0], far_turned[...]),
    )
    for k, (one, two) in enumerate(pairs):
        out_ref[slots[k]] = (one.astype(jnp.float32) + two.astype(jnp.float32)).astype(jnp.bfloat16)


def add_up(slots, *parts):
    whole = pl.BlockSpec(memory_space=pltpu.VMEM)
    return pl.pallas_call(
        sum_kernel,
        out_shape=jax.ShapeDtypeStruct((6, B, B), jnp.bfloat16),
        in_specs=[pl.BlockSpec(memory_space=pltpu.SMEM)] + [whole] * len(parts),
        out_specs=whole,
        compiler_params=pltpu.CompilerParams(vmem_limit_bytes=40 * MIB),
        cost_estimate=pl.CostEstimate(flops=6 * B * B, bytes_accessed=9 * MIB, transcendentals=0),
        name="add_up",
    )(slots, *parts)


def local(features, sources):
    me = lax.axis_index("blk")
    odd = me % 2
    place = (me - SEAM_AT) % SEAM
    spot = me % PLANE
    side = jnp.where(spot < 2, 1, jnp.where(spot >= PLANE - 2, 2, 0))
    own_half = ((me - SEAM_AT) % N) // SEAM
    tags = (sources[:, None] == jnp.arange(TAG, dtype=sources.dtype)[None, :]).astype(jnp.bfloat16)
    keep, other, ahead = make_units(features, tags, own_half, ((me - 2 - SEAM_AT) % N) // SEAM)

    def place_of(i):
        return (i - SEAM_AT) % SEAM

    after2 = send(ahead, lambda i: i - 2, lambda i: border_side(i) != 1)
    before2 = send(keep, lambda i: i + 2, lambda i: border_side(i) != 2)
    first, second = border_routes()
    crossed_once = lax.ppermute(keep, "blk", first)
    second_half = send(
        keep,
        lambda i: i - PLANE if place_of(i) == 1 else i + SEAM,
        lambda i: place_of(i) < 3,
    )
    opposite = send(hold(other, crossed_once), lambda i: i + SEAM)
    crossed_twice = lax.ppermute(crossed_once, "blk", second)
    edge = lax.ppermute(jnp.where(place == 2, other, crossed_once), "blk", edge_routes())
    mate = send(hold(keep, after2, before2, opposite, second_half, crossed_twice), lambda i: i ^ 1)
    after2, before2, mate = lax.optimization_barrier((after2, before2, mate))
    after2, before2 = merge(side, odd, crossed_twice, crossed_once, after2, before2)
    before3 = send(before2, lambda i: i + 1, lambda i: i % 2 == 1 and i % PLANE != PLANE - 1)
    after3 = send(after2, lambda i: i - 1, lambda i: i % 2 == 0 and i % PLANE != 0 and place_of(i) != 0)
    after_mate = send(after2, lambda i: i ^ 1)
    before_mate = send(before2, lambda i: i ^ 1)
    second_round = send(hold(second_half, mate), lambda i: i - PLANE, lambda i: place_of(i + PLANE) == 1)

    zero = jnp.zeros((), jnp.int32)
    seam = jnp.where(place == 0, 1, jnp.where(place == 1, 2, 0))
    near, turned1, turned2, crossed = tiles(
        [opposite, second_half, second_round],
        [[after2], [before2], [mate], [after_mate], [before_mate]],
        seam,
        [zero] * 5,
        (1, 4),
        (2, 3, 4),
    )
    far_choice = jnp.where((spot == 0) | (spot == PLANE - 1) | (place == SEAM - 1), 2, odd)
    far, far_turned = tiles(
        [hold(opposite, near), second_half],
        [[before3, after3, edge]],
        jnp.where((odd == 0) & (place < 3), 1, 0),
        [far_choice],
        (0,),
    )

    near = send(near, lambda i: i + SEAM)
    far = send(far, lambda i: i + SEAM)
    crossed = send(crossed, lambda i: i ^ 1)
    turned1, turned2, crossed = hold(turned1, before3, after3), hold(turned2, before3, after3), crossed
    up = send(jnp.stack([turned1, crossed[1]]), lambda i: i + 2)
    down = send(jnp.stack([turned2, crossed[2]]), lambda i: i - 2)
    far_turned = send(far_turned, lambda i: i + 3 if i % 2 else i - 3)
    slots = jnp.where(odd == 1, jnp.array([4, 3, 2, 5, 0, 1], jnp.int32), jnp.array([5, 3, 2, 1, 4, 0], jnp.int32))
    return jnp.transpose(add_up(slots, near, far, crossed, up, down, far_turned), (1, 0, 2))


def solution(mesh):
    return jax.shard_map(
        local,
        mesh=mesh,
        in_specs=(P("blk", None), P("blk")),
        out_specs=P("blk", None, None),
        check_vma=False,
    )
```

time: 357 us -> 330 us (0.924); the launches traced: 357 us -> 324 us
  starting transfers between devices: 56.1 us -> 34.3 us
  waiting for transfers between devices: 241 us -> 224 us
  other arithmetic: 3.14 us -> 8.12 us
  local copies, waits for them, and re-layouts: 6.04 us -> 10.8 us
  Pallas kernels: 50.5 us -> 46.5 us
    ppermute x3, waiting for transfers between devices: 97.2 us -> 40.3 us  [the longest x1 40.3 us: local(): crossed_once = lax.ppermute(keep, 'blk', first)]
    ppermute x20 -> x16, waiting for transfers between devices: 143 us -> 184 us  [send(): return lax.ppermute(block, 'blk', pairs)]
    ppermute x20 -> x16, starting transfers between devices: 39.7 us -> 17.7 us  [send(): return lax.ppermute(block, 'blk', pairs)]
    unnamed x8 -> x16, local copies, waits for them, and re-layouts: 2.5 us -> 10.7 us
    select_n x0 -> x1, other arithmetic: none -> 4.83 us  [local(): jnp.where(place == 2, other, crossed_once)]
    pallas_call x3 -> x2, Pallas kernels: 32 us -> 29 us  [tiles(): pl.pallas_call(kernel, out_shape=outs, in_specs=[pl.BlockSpec(memory_spac...]
  transfers between devices with their start and end apart: 23 -> 19, of which waited for: 11 -> 7; matrix products, arithmetic and copies ran while one was open for 2% -> 2% of each run, Pallas kernels for 10% -> 9%
where the time goes in v3:
time: 330 us; the launch traced here: 324 us
  waiting for transfers between devices  224 us (68%)
  Pallas kernels  46.5 us (14%)
  starting transfers between devices  34.3 us (10%)
  local copies, waits for them, and re-layouts  10.8 us (3%)
  other arithmetic  8.12 us (2%)
    ppermute x16, waiting for transfers between devices, send(): return lax.ppermute(block, 'blk', pairs)  184 us
    ppermute x1, waiting for transfers between devices, local(): crossed_once = lax.ppermute(keep, 'blk', first)  40.3 us
    pallas_call x2, Pallas kernels, tiles(): pl.pallas_call(kernel, out_shape=outs, in_specs=[pl.BlockSpec(memory_spac...  29 us
    ppermute x16, starting transfers between devices, send(): return lax.ppermute(block, 'blk', pairs)  17.7 us
    ppermute x1, starting transfers between devices, local(): crossed_once = lax.ppermute(keep, 'blk', first)  12.9 us
    unnamed x16, local copies, waits for them, and re-layouts  10.7 us
    pallas_call x1, Pallas kernels, make_units(): pl.pallas_call(unit_kernel, out_shape=(out, out, out), grid_spec=pltpu.Pr...  9.93 us
  transfers between devices with their start and end apart: 19, of which 7 were waited for; matrix products, arithmetic and copies ran while one was open for 2% of the time, Pallas kernels for 9%

profile of v3, /device:TPU:1, one launch (start us, length us, event | category | flops | bytes accessed | tf_op | source)
XLA Modules:
  0.0 324.3 jit_solution(4240818352307336122)
XLA Ops:
  0.9 9.9 %units.1 = (bf16[512,4224]{1,0:T(8,128)(2,1)}, bf16[512,4224]{1,0:T(8,128)(2,1)S(1)}, bf16[512,4224]{1,0:T(8,128)(2,1)S(1)}) custom-call(s32[2]{0:T(128)S(1)} %pad_add_fusion.1.info, bf16[512,8192]{1,0:T(8,128)(2,1)} %x_ref.1, bf16[512,128]{1,0:T(8,128)(2,1)S(1)} %fusion.tag_ref), custom_call_target="tpu_custom_call" | custom-call | flops 25165824 | bytes 20971520 | tf_op jit(solution)/shard_map/units/pallas_call | solution.py:85
  10.8 12.9 %collective-permute-start = (bf16[512,4224]{1,0:T(8,128)(2,1)}, bf16[512,4224]{1,0:T(8,128)(2,1)S(1)}, u32[]{:S(2)}, u32[]{:S(2)}) collective-permute-start(bf16[512,4224]{1,0:T(8,128)(2,1)} %get-tuple-element.29), channel_id=1, source_target_pairs={{1,255},{63,65},{0,192},{62,126},{61,125},{2,194},{65,63},{127,129... | collective-permute-start | bytes 12976136 | tf_op jit(solution)/shard_map/ppermute | solution.py:274
  23.8 2.7 collective-permute-start.2
  26.5 3.3 %collective-permute-start.4 = (bf16[512,4224]{1,0:T(8,128)(2,1)}, bf16[512,4224]{1,0:T(8,128)(2,1)}, u32[]{:S(2)}, u32[]{:S(2)}) collective-permute-start(bf16[512,4224]{1,0:T(8,128)(2,1)} %get-tuple-element.29), channel_id=1, source_target_pairs={{0,2},{1,3},{2,4},{3,5},{4,6},{5,7},{6,8},{7,9},{8,10},{9,11},{10,... | collective-permute-start | bytes 12976136 | tf_op jit(solution)/shard_map/ppermute | solution.py:23
  31.1 40.3 %collective-permute-done.odd = bf16[512,4224]{1,0:T(8,128)(2,1)S(1)} collective-permute-done((bf16[512,4224]{1,0:T(8,128)(2,1)}, bf16[512,4224]{1,0:T(8,128)(2,1)S(1)}, u32[]{:S(2)}, u32[]{:S(2)}) %collective-permute-start) | collective-permute-done | bytes 4325408 | tf_op jit(solution)/shard_map/ppermute | solution.py:274
  72.6 2.1 copy-done
  74.6 48.5 %collective-permute-done.3.after_in = bf16[512,4224]{1,0:T(8,128)(2,1)} collective-permute-done((bf16[512,4224]{1,0:T(8,128)(2,1)S(1)}, bf16[512,4224]{1,0:T(8,128)(2,1)}, u32[]{:S(2)}, u32[]{:S(2)}) %collective-permute-start.3) | collective-permute-done | bytes 4325408 | tf_op jit(solution)/shard_map/ppermute | solution.py:23
  123.1 41.1 %collective-permute-done.1.refs_0_ = bf16[512,4224]{1,0:T(8,128)(2,1)S(1)} collective-permute-done((bf16[512,4224]{1,0:T(8,128)(2,1)S(1)}, bf16[512,4224]{1,0:T(8,128)(2,1)S(1)}, u32[]{:S(2)}, u32[]{:S(2)}) %collective-permute-start.1) | collective-permute-done | bytes 4325408 | tf_op jit(solution)/shard_map/ppermute | solution.py:23
  164.2 2.1 copy-done.5
  166.2 2.1 copy-done.3
  168.4 7.6 %collective-permute-done.6.refs_5_ = bf16[512,4224]{1,0:T(8,128)(2,1)} collective-permute-done((bf16[512,4224]{1,0:T(8,128)(2,1)}, bf16[512,4224]{1,0:T(8,128)(2,1)}, u32[]{:S(2)}, u32[]{:S(2)}) %collective-permute-start.6) | collective-permute-done | bytes 4325408 | tf_op jit(solution)/shard_map/ppermute | solution.py:23
  176.0 2.2 copy-done.1
  178.3 2.2 copy-done.4
  180.5 3.1 merge.1
  184.2 2.8 collective-permute-start.7
  186.9 3.4 %collective-permute-start.11 = (bf16[512,4224]{1,0:T(8,128)(2,1)}, bf16[512,4224]{1,0:T(8,128)(2,1)}, u32[]{:S(2)}, u32[]{:S(2)}) collective-permute-start(bf16[512,4224]{1,0:T(8,128)(2,1)} %get-tuple-element.35.refs_4_), channel_id=1, source_target_pairs={{1,2},{3,4},{5,6},{7,8},{9,10},{11,12},{13,14},{15,16},{17,18},{19... | collective-permute-start | bytes 12976136 | tf_op jit(solution)/shard_map/ppermute | solution.py:23
  191.6 4.8 %broadcast_select_fusion = bf16[512,4224]{1,0:T(8,128)(2,1)} fusion(bf16[512,4224]{1,0:T(8,128)(2,1)} %copy-done.2, bf16[512,4224]{1,0:T(8,128)(2,1)} %copy-done, pred[]{:T(512)S(6)} %eq.53), kind=kLoop, calls=%fused_computation | loop fusion | flops 2162688 | bytes 12976129 | tf_op jit(solution)/shard_map/jit(_where)/select_n | solution.py:282
  196.5 2.7 collective-permute-start.13
  199.2 21.1 %tiles.2 = (bf16[5,512,512]{2,1,0:T(8,128)(2,1)}, bf16[512,512]{1,0:T(8,128)(2,1)S(1)}, bf16[512,512]{1,0:T(8,128)(2,1)S(1)}, bf16[3,512,512]{2,1,0:T(8,128)(2,1)S(1)}) custom-call(s32[6]{0:T(128)S(1)} %pad_add_fusion.info, bf16[512,4224]{1,0:T(8,128)(2,1)} %copy-done.5, bf16[512,4224]{1,0:T(8,128)(2,1)} %collective-permute-done.2.refs_1_, ...), custom_call_target="tpu_custom_call" | custom-call | flops 10737418240 | bytes 25165824 | tf_op jit(solution)/shard_map/tiles/pallas_call | solution.py:179
  220.7 14.7 %collective-permute-done.11.refs_2_ = bf16[512,4224]{1,0:T(8,128)(2,1)} collective-permute-done((bf16[512,4224]{1,0:T(8,128)(2,1)}, bf16[512,4224]{1,0:T(8,128)(2,1)}, u32[]{:S(2)}, u32[]{:S(2)}) %collective-permute-start.11) | collective-permute-done | bytes 4325408 | tf_op jit(solution)/shard_map/ppermute | solution.py:23
  235.4 12.4 %collective-permute-done.12.refs_3_ = bf16[512,4224]{1,0:T(8,128)(2,1)} collective-permute-done((bf16[512,4224]{1,0:T(8,128)(2,1)}, bf16[512,4224]{1,0:T(8,128)(2,1)}, u32[]{:S(2)}, u32[]{:S(2)}) %collective-permute-start.12) | collective-permute-done | bytes 4325408 | tf_op jit(solution)/shard_map/ppermute | solution.py:23
  251.6 7.9 %tiles.3 = (bf16[1,512,512]{2,1,0:T(8,128)(2,1)}, bf16[512,512]{1,0:T(8,128)(2,1)}) custom-call(s32[2]{0:T(128)S(1)} %pad_add_fusion.3.info, bf16[512,4224]{1,0:T(8,128)(2,1)} %copy-done.5, bf16[512,4224]{1,0:T(8,128)(2,1)} %collective-permute-done.2.refs_1_, bf16[512,4224]{1,0:T(8,128)(2,1)} %collective-permute-done.11.refs_2_, ...), custom_call_target="tpu_custom_call" | custom-call | flops 2147483648 | bytes 8388608 | tf_op jit(solution)/shard_map/tiles/pallas_call | solution.py:179
  259.8 59.9 %collective-permute-done.14.far = bf16[1,512,512]{2,1,0:T(8,128)(2,1)S(1)} collective-permute-done((bf16[1,512,512]{2,1,0:T(8,128)(2,1)}, bf16[1,512,512]{2,1,0:T(8,128)(2,1)S(1)}, u32[]{:S(2)}, u32[]{:S(2)}) %collective-permute-start.14) | collective-permute-done | bytes 524320 | tf_op jit(solution)/shard_map/ppermute | solution.py:23
  319.8 4.5 %add_up.1 = bf16[6,512,512]{2,1,0:T(8,128)(2,1)} custom-call(s32[6]{0:T(128)S(1)} %broadcast_select_fusion.1.slots, bf16[5,512,512]{2,1,0:T(8,128)(2,1)} %collective-permute-done.10.near, bf16[1,512,512]{2,1,0:T(8,128)(2,1)S(1)} %collective-permute-done.14.far, bf16[3,512,512]{2,1,0:T(8,128)(2,1)S(1)} %collective-permute-done.15.crossed, ...), custom_call_target="tpu_custom_call" | custom-call | flops 1572864 | bytes 9437184 | tf_op jit(solution)/shard_map/add_up/pallas_call | solution.py:247
  (46 shorter events, 9.9 us)
Async XLA Ops:
  10.8 153.3 %copy-start.2 = (bf16[512,4224]{1,0:T(8,128)(2,1)}, bf16[512,4224]{1,0:T(8,128)(2,1)S(1)}, u32[]{:S(2)}) copy-start(bf16[512,4224]{1,0:T(8,128)(2,1)S(1)} %get-tuple-element.27) | copy-start | bytes 12976132
  10.8 60.5 %collective-permute-start = (bf16[512,4224]{1,0:T(8,128)(2,1)}, bf16[512,4224]{1,0:T(8,128)(2,1)S(1)}, u32[]{:S(2)}, u32[]{:S(2)}) collective-permute-start(bf16[512,4224]{1,0:T(8,128)(2,1)} %get-tuple-element.29), channel_id=1, source_target_pairs={{1,255},{63,65},{0,192},{62,126},{61,125},{2,194},{65,63},{127,129... | collective-permute-start | bytes 12976136 | tf_op jit(solution)/shard_map/ppermute | solution.py:274
  23.8 50.8 %collective-permute-start.2 = (bf16[512,4224]{1,0:T(8,128)(2,1)}, bf16[512,4224]{1,0:T(8,128)(2,1)}, u32[]{:S(2)}, u32[]{:S(2)}) collective-permute-start(bf16[512,4224]{1,0:T(8,128)(2,1)} %get-tuple-element.29), channel_id=1, source_target_pairs={{32,160},{33,225},{34,162},{160,32},{161,97},{162,34}} | collective-permute-start | bytes 12976136 | tf_op jit(solution)/shard_map/ppermute | solution.py:23
  26.5 96.6 %collective-permute-start.4 = (bf16[512,4224]{1,0:T(8,128)(2,1)}, bf16[512,4224]{1,0:T(8,128)(2,1)}, u32[]{:S(2)}, u32[]{:S(2)}) collective-permute-start(bf16[512,4224]{1,0:T(8,128)(2,1)} %get-tuple-element.29), channel_id=1, source_target_pairs={{0,2},{1,3},{2,4},{3,5},{4,6},{5,7},{6,8},{7,9},{8,10},{9,11},{10,... | collective-permute-start | bytes 12976136 | tf_op jit(solution)/shard_map/ppermute | solution.py:23
  29.8 93.3 %collective-permute-start.3 = (bf16[512,4224]{1,0:T(8,128)(2,1)S(1)}, bf16[512,4224]{1,0:T(8,128)(2,1)}, u32[]{:S(2)}, u32[]{:S(2)}) collective-permute-start(bf16[512,4224]{1,0:T(8,128)(2,1)S(1)} %get-tuple-element.28), channel_id=1, source_target_pairs={{2,0},{3,1},{4,2},{5,3},{6,4},{7,5},{8,6},{9,7},{10,8},{11,9},{12,... | collective-permute-start | bytes 12976136 | tf_op jit(solution)/shard_map/ppermute | solution.py:23
  71.4 92.8 %collective-permute-start.1 = (bf16[512,4224]{1,0:T(8,128)(2,1)S(1)}, bf16[512,4224]{1,0:T(8,128)(2,1)S(1)}, u32[]{:S(2)}, u32[]{:S(2)}) collective-permute-start(bf16[512,4224]{1,0:T(8,128)(2,1)S(1)} %get-tuple-element.27), channel_id=1, source_target_pairs={{0,128},{1,129},{2,130},{3,131},{4,132},{5,133},{6,134},{7,135},{8... | collective-permute-start | bytes 12976136 | tf_op jit(solution)/shard_map/ppermute | solution.py:23
  71.6 92.5 %collective-permute-start.5 = (bf16[512,4224]{1,0:T(8,128)(2,1)S(1)}, bf16[512,4224]{1,0:T(8,128)(2,1)S(1)}, u32[]{:S(2)}, u32[]{:S(2)}) collective-permute-start(bf16[512,4224]{1,0:T(8,128)(2,1)S(1)} %collective-permute-done.odd), channel_id=1, source_target_pairs={{0,62},{62,0},{64,126},{126,64},{128,190},{190,128},{192,254},{254... | collective-permute-start | bytes 12976136 | tf_op jit(solution)/shard_map/ppermute | solution.py:281
  168.3 7.7 %collective-permute-start.6 = (bf16[512,4224]{1,0:T(8,128)(2,1)}, bf16[512,4224]{1,0:T(8,128)(2,1)}, u32[]{:S(2)}, u32[]{:S(2)}) collective-permute-start(bf16[512,4224]{1,0:T(8,128)(2,1)} %get-tuple-element.29), channel_id=1, source_target_pairs={{0,1},{1,0},{2,3},{3,2},{4,5},{5,4},{6,7},{7,6},{8,9},{9,8},{10,11... | collective-permute-start | bytes 12976136 | tf_op jit(solution)/shard_map/ppermute | solution.py:23
  176.0 2.2 copy-start.1
  178.3 2.2 copy-start.4
  183.6 12.9 %collective-permute-start.8 = (bf16[512,4224]{1,0:T(8,128)(2,1)}, bf16[512,4224]{1,0:T(8,128)(2,1)}, u32[]{:S(2)}, u32[]{:S(2)}) collective-permute-start(bf16[512,4224]{1,0:T(8,128)(2,1)} %get-tuple-element.34.refs_3_), channel_id=1, source_target_pairs={{0,1},{1,0},{2,3},{3,2},{4,5},{5,4},{6,7},{7,6},{8,9},{9,8},{10,11... | collective-permute-start | bytes 12976136 | tf_op jit(solution)/shard_map/ppermute | solution.py:23
  183.8 15.5 %collective-permute-start.9 = (bf16[512,4224]{1,0:T(8,128)(2,1)}, bf16[512,4224]{1,0:T(8,128)(2,1)}, u32[]{:S(2)}, u32[]{:S(2)}) collective-permute-start(bf16[512,4224]{1,0:T(8,128)(2,1)} %get-tuple-element.35.refs_4_), channel_id=1, source_target_pairs={{0,1},{1,0},{2,3},{3,2},{4,5},{5,4},{6,7},{7,6},{8,9},{9,8},{10,11... | collective-permute-start | bytes 12976136 | tf_op jit(solution)/shard_map/ppermute | solution.py:23
  184.2 15.1 %collective-permute-start.7 = (bf16[512,4224]{1,0:T(8,128)(2,1)}, bf16[512,4224]{1,0:T(8,128)(2,1)}, u32[]{:S(2)}, u32[]{:S(2)}) collective-permute-start(bf16[512,4224]{1,0:T(8,128)(2,1)} %collective-permute-done.2.refs_1_), channel_id=1, source_target_pairs={{97,33},{225,161}} | collective-permute-start | bytes 12976136 | tf_op jit(solution)/shard_map/ppermute | solution.py:23
  186.9 48.4 %collective-permute-start.11 = (bf16[512,4224]{1,0:T(8,128)(2,1)}, bf16[512,4224]{1,0:T(8,128)(2,1)}, u32[]{:S(2)}, u32[]{:S(2)}) collective-permute-start(bf16[512,4224]{1,0:T(8,128)(2,1)} %get-tuple-element.35.refs_4_), channel_id=1, source_target_pairs={{1,2},{3,4},{5,6},{7,8},{9,10},{11,12},{13,14},{15,16},{17,18},{19... | collective-permute-start | bytes 12976136 | tf_op jit(solution)/shard_map/ppermute | solution.py:23
  190.3 57.4 %collective-permute-start.12 = (bf16[512,4224]{1,0:T(8,128)(2,1)}, bf16[512,4224]{1,0:T(8,128)(2,1)}, u32[]{:S(2)}, u32[]{:S(2)}) collective-permute-start(bf16[512,4224]{1,0:T(8,128)(2,1)} %get-tuple-element.34.refs_3_), channel_id=1, source_target_pairs={{2,1},{4,3},{6,5},{8,7},{10,9},{12,11},{14,13},{16,15},{18,17},{20... | collective-permute-start | bytes 12976136 | tf_op jit(solution)/shard_map/ppermute | solution.py:23
  196.5 55.1 %collective-permute-start.13 = (bf16[512,4224]{1,0:T(8,128)(2,1)}, bf16[512,4224]{1,0:T(8,128)(2,1)}, u32[]{:S(2)}, u32[]{:S(2)}) collective-permute-start(bf16[512,4224]{1,0:T(8,128)(2,1)} %broadcast_select_fusion), channel_id=1, source_target_pairs={{61,0},{2,63},{125,64},{66,127},{189,128},{130,191},{253,192},{194... | collective-permute-start | bytes 12976136 | tf_op jit(solution)/shard_map/ppermute | solution.py:282
  220.4 27.4 %collective-permute-start.15 = (bf16[3,512,512]{2,1,0:T(8,128)(2,1)S(1)}, bf16[3,512,512]{2,1,0:T(8,128)(2,1)S(1)}, u32[]{:S(2)}, u32[]{:S(2)}) collective-permute-start(bf16[3,512,512]{2,1,0:T(8,128)(2,1)S(1)} %get-tuple-element.39), channel_id=1, source_target_pairs={{0,1},{1,0},{2,3},{3,2},{4,5},{5,4},{6,7},{7,6},{8,9},{9,8},{10,11... | collective-permute-start | bytes 4718600 | tf_op jit(solution)/shard_map/ppermute | solution.py:23
  220.5 99.3 %collective-permute-start.10 = (bf16[5,512,512]{2,1,0:T(8,128)(2,1)}, bf16[5,512,512]{2,1,0:T(8,128)(2,1)}, u32[]{:S(2)}, u32[]{:S(2)}) collective-permute-start(bf16[5,512,512]{2,1,0:T(8,128)(2,1)} %get-tuple-element.36), channel_id=1, source_target_pairs={{0,128},{1,129},{2,130},{3,131},{4,132},{5,133},{6,134},{7,135},{8... | collective-permute-start | bytes 7864328 | tf_op jit(solution)/shard_map/ppermute | solution.py:23
  249.0 70.8 %collective-permute-start.17 = (bf16[2,512,512]{2,1,0:T(8,128)(2,1)}, bf16[2,512,512]{2,1,0:T(8,128)(2,1)S(1)}, u32[]{:S(2)}, u32[]{:S(2)}) collective-permute-start(bf16[2,512,512]{2,1,0:T(8,128)(2,1)} %pad_maximum_fusion.1), channel_id=1, source_target_pairs={{0,254},{1,255},{2,0},{3,1},{4,2},{5,3},{6,4},{7,5},{8,6},{9,7},{1... | collective-permute-start | bytes 3145736 | tf_op jit(solution)/shard_map/ppermute | solution.py:23
  250.0 69.7 %collective-permute-start.16 = (bf16[2,512,512]{2,1,0:T(8,128)(2,1)}, bf16[2,512,512]{2,1,0:T(8,128)(2,1)}, u32[]{:S(2)}, u32[]{:S(2)}) collective-permute-start(bf16[2,512,512]{2,1,0:T(8,128)(2,1)} %pad_maximum_fusion), channel_id=1, source_target_pairs={{0,2},{1,3},{2,4},{3,5},{4,6},{5,7},{6,8},{7,9},{8,10},{9,11},{10,... | collective-permute-start | bytes 3145736 | tf_op jit(solution)/shard_map/ppermute | solution.py:23
  251.6 8.2 %copy-start.6 = (s32[6]{0:T(128)S(1)}, s32[6]{0:T(128)}, u32[]{:S(2)}) copy-start(s32[6]{0:T(128)} %constant.92.clone) | copy-start | bytes 76
  251.6 8.2 %copy-start.7 = (s32[6]{0:T(128)S(1)}, s32[6]{0:T(128)}, u32[]{:S(2)}) copy-start(s32[6]{0:T(128)} %constant.93.clone) | copy-start | bytes 76
  259.5 60.3 %collective-permute-start.14 = (bf16[1,512,512]{2,1,0:T(8,128)(2,1)}, bf16[1,512,512]{2,1,0:T(8,128)(2,1)S(1)}, u32[]{:S(2)}, u32[]{:S(2)}) collective-permute-start(bf16[1,512,512]{2,1,0:T(8,128)(2,1)} %get-tuple-element.38), channel_id=1, source_target_pairs={{0,128},{1,129},{2,130},{3,131},{4,132},{5,133},{6,134},{7,135},{8... | collective-permute-start | bytes 1572872 | tf_op jit(solution)/shard_map/ppermute | solution.py:23
  259.6 60.2 %collective-permute-start.18 = (bf16[512,512]{1,0:T(8,128)(2,1)}, bf16[512,512]{1,0:T(8,128)(2,1)}, u32[]{:S(2)}, u32[]{:S(2)}) collective-permute-start(bf16[512,512]{1,0:T(8,128)(2,1)} %get-tuple-element.44), channel_id=1, source_target_pairs={{0,253},{1,4},{2,255},{3,6},{4,1},{5,8},{6,3},{7,10},{8,5},{9,12},... | collective-permute-start | bytes 1572872 | tf_op jit(solution)/shard_map/ppermute | solution.py:23
  (3 other events, 6.2 us)

commit v4 on v3

--- a/solution.py
+++ b/solution.py
@@ -100,7 +100,7 @@
     )(jnp.stack([own_half, ahead_half]).astype(jnp.int32), features, tags)
 
 
-def tiles(rows, blocks, row_choice, block_choice, seam_tiles, stacked=()):
+def tiles(rows, blocks, row_choice, block_choice, seam_tiles, stacked=(), short=False):
     count = len(blocks)
     used_rows = len(rows)
     blocks = [[option if isinstance(option, tuple) else (option,) for option in entry] for entry in blocks]
@@ -190,7 +190,9 @@
         ],
         compiler_params=pltpu.CompilerParams(vmem_limit_bytes=50 * MIB),
         cost_estimate=pl.CostEstimate(
-            flops=2 * count * B * B * HALF, bytes_accessed=4 * MIB * (1 + count), transcendentals=0
+            flops=0 if short else 2 * count * B * B * HALF,
+            bytes_accessed=MIB if short else 4 * MIB * (1 + count),
+            transcendentals=0,
         ),
         name="tiles",
     )(info, *rows, *flat)
@@ -201,16 +203,18 @@
         for core, source in ((0, even), (1, odd)):
             @pl.when((info[0] == side) & (info[1] == core))
             def _(ref=ref, source=source):
-                for out in (False, True):
-                    copies = []
-                    for k in range(4):
-                        rows = pl.ds(k * B // 4, B // 4)
-                        pair = (held.at[rows], ref.at[rows]) if out else (source.at[rows], held.at[rows])
-                        copies.append(pltpu.make_async_copy(*pair, sems.at[k]))
-                    for copy in copies:
-                        copy.start()
-                    for copy in copies:
-                        copy.wait()
+                into, out = [], []
+                for k in range(8):
+                    rows = pl.ds(k * B // 8, B // 8)
+                    into.append(pltpu.make_async_copy(source.at[rows], held.at[rows], sems.at[k]))
+                    out.append(pltpu.make_async_copy(held.at[rows], ref.at[rows], sems.at[8 + k]))
+                for copy in into:
+                    copy.start()
+                for k in range(8):
+                    into[k].wait()
+                    out[k].start()
+                for copy in out:
+                    copy.wait()
 
 
 def merge(side, core, even, odd, after, before):
@@ -221,7 +225,7 @@
         out_shape=(out, out),
         in_specs=[pl.BlockSpec(memory_space=pltpu.SMEM)] + [whole] * 4,
         out_specs=(whole, whole),
-        scratch_shapes=[pltpu.VMEM((B, WIDE), jnp.bfloat16), pltpu.SemaphoreType.DMA((4,))],
+        scratch_shapes=[pltpu.VMEM((B, WIDE), jnp.bfloat16), pltpu.SemaphoreType.DMA((16,))],
         input_output_aliases={3: 0, 4: 1},
         compiler_params=pltpu.CompilerParams(vmem_limit_bytes=16 * MIB),
         cost_estimate=pl.CostEstimate(flops=0, bytes_accessed=MIB, transcendentals=0),
@@ -229,13 +233,13 @@
     )(jnp.stack([side, core]).astype(jnp.int32), even, odd, after, before)
 
 
-def sum_kernel(slots, near, far, crossed, up, down, far_turned, out_ref):
+def sum_kernel(slots, near, mid, far, crossed, up, down, far_turned, out_ref):
     pairs = (
-        (near[2], crossed[0]),
-        (near[0], down[0]),
-        (near[1], up[0]),
-        (near[3], down[1]),
-        (near[4], up[1]),
+        (near[0], crossed[0]),
+        (near[1], down[0]),
+        (mid[0], up[0]),
+        (mid[1], down[1]),
+        (mid[2], up[1]),
         (far[0], far_turned[...]),
     )
     for k, (one, two) in enumerate(pairs):
@@ -279,29 +283,37 @@
     )
     opposite = send(hold(other, crossed_once), lambda i: i + SEAM)
     crossed_twice = lax.ppermute(crossed_once, "blk", second)
-    edge = lax.ppermute(jnp.where(place == 2, other, crossed_once), "blk", edge_routes())
     mate = send(hold(keep, after2, before2, opposite, second_half, crossed_twice), lambda i: i ^ 1)
-    after2, before2, mate = lax.optimization_barrier((after2, before2, mate))
+    second_round = send(
+        hold(second_half, after2, before2, opposite), lambda i: i - PLANE, lambda i: place_of(i + PLANE) == 1
+    )
+    edge = jnp.where(place == 2, other, crossed_once)
+    after2, before2, mate, edge = lax.optimization_barrier((after2, before2, mate, edge))
     after2, before2 = merge(side, odd, crossed_twice, crossed_once, after2, before2)
     before3 = send(before2, lambda i: i + 1, lambda i: i % 2 == 1 and i % PLANE != PLANE - 1)
     after3 = send(after2, lambda i: i - 1, lambda i: i % 2 == 0 and i % PLANE != 0 and place_of(i) != 0)
     after_mate = send(after2, lambda i: i ^ 1)
     before_mate = send(before2, lambda i: i ^ 1)
-    second_round = send(hold(second_half, mate), lambda i: i - PLANE, lambda i: place_of(i + PLANE) == 1)
 
     zero = jnp.zeros((), jnp.int32)
     seam = jnp.where(place == 0, 1, jnp.where(place == 1, 2, 0))
-    near, turned1, turned2, crossed = tiles(
-        [opposite, second_half, second_round],
-        [[after2], [before2], [mate], [after_mate], [before_mate]],
+    rows = [opposite, second_half, second_round]
+    rows = [opposite, second_half, second_round]
+    near, turned0, turned1 = tiles(rows[:1], [[mate], [after2]], zero, [zero] * 2, ())
+    edge = lax.ppermute(hold(edge, turned1), "blk", edge_routes())
+    mid, turned2, crossed = tiles(
+        [hold(opposite, near)] + rows[1:],
+        [[before2], [after_mate], [before_mate]],
         seam,
-        [zero] * 5,
-        (1, 4),
-        (2, 3, 4),
-    )
+        [zero] * 3,
+        (0, 2),
+        (1, 2),
+        True,
+    )
+    crossed = jnp.concatenate([turned0[None], crossed])
     far_choice = jnp.where((spot == 0) | (spot == PLANE - 1) | (place == SEAM - 1), 2, odd)
     far, far_turned = tiles(
-        [hold(opposite, near), second_half],
+        [hold(opposite, mid), second_half],
         [[before3, after3, edge]],
         jnp.where((odd == 0) & (place < 3), 1, 0),
         [far_choice],
@@ -309,6 +321,8 @@
     )
 
     near = send(near, lambda i: i + SEAM)
+    mid = send(mid, lambda i: i + SEAM)
+    crossed = hold(crossed, near)
     far = send(far, lambda i: i + SEAM)
     crossed = send(crossed, lambda i: i ^ 1)
     turned1, turned2, crossed = hold(turned1, before3, after3), hold(turned2, before3, after3), crossed
@@ -316,7 +330,7 @@
     down = send(jnp.stack([turned2, crossed[2]]), lambda i: i - 2)
     far_turned = send(far_turned, lambda i: i + 3 if i % 2 else i - 3)
     slots = jnp.where(odd == 1, jnp.array([4, 3, 2, 5, 0, 1], jnp.int32), jnp.array([5, 3, 2, 1, 4, 0], jnp.int32))
-    return jnp.transpose(add_up(slots, near, far, crossed, up, down, far_turned), (1, 0, 2))
+    return jnp.transpose(add_up(slots, near, mid, far, crossed, up, down, far_turned), (1, 0, 2))
 
 
 def solution(mesh):

time: 330 us -> 312 us (0.945); the launches traced: 324 us -> 312 us
  waiting for transfers between devices: 224 us -> 208 us
    ppermute x16 -> x17, waiting for transfers between devices: 184 us -> 166 us  [send(): return lax.ppermute(block, 'blk', pairs)]
    pallas_call x2 -> x3, Pallas kernels: 29 us -> 31.5 us  [tiles(): pl.pallas_call(kernel, out_shape=outs, in_specs=[pl.BlockSpec(memory_spac...]
    unnamed x16 -> x34, local copies, waits for them, and re-layouts: 10.7 us -> 11.2 us
    ppermute x16 -> x17, starting transfers between devices: 17.7 us -> 17.8 us  [send(): return lax.ppermute(block, 'blk', pairs)]
  transfers between devices with their start and end apart: 19 -> 20, of which waited for: 7 -> 7; matrix products, arithmetic and copies ran while one was open for 2% -> 3% of each run, Pallas kernels for 9% -> 11%
where the time goes in v4:
time: 312 us
  waiting for transfers between devices  208 us (67%)
  Pallas kernels  48.7 us (16%)
  starting transfers between devices  34.7 us (11%)
  local copies, waits for them, and re-layouts  11.2 us (4%)
  other arithmetic  8.79 us (3%)
    ppermute x17, waiting for transfers between devices, send(): return lax.ppermute(block, 'blk', pairs)  166 us
    ppermute x1, waiting for transfers between devices, local(): crossed_once = lax.ppermute(keep, 'blk', first)  42 us
    pallas_call x3, Pallas kernels, tiles(): pl.pallas_call(kernel, out_shape=outs, in_specs=[pl.BlockSpec(memory_spac...  31.5 us
    ppermute x17, starting transfers between devices, send(): return lax.ppermute(block, 'blk', pairs)  17.8 us
    ppermute x1, starting transfers between devices, local(): crossed_once = lax.ppermute(keep, 'blk', first)  12.9 us
    unnamed x34, local copies, waits for them, and re-layouts  11.2 us
    pallas_call x1, Pallas kernels, make_units(): pl.pallas_call(unit_kernel, out_shape=(out, out, out), grid_spec=pltpu.Pr...  9.91 us
  transfers between devices with their start and end apart: 20, of which 7 were waited for; matrix products, arithmetic and copies ran while one was open for 3% of the time, Pallas kernels for 11%

profile of v4, /device:TPU:1, one launch (start us, length us, event | category | flops | bytes accessed | tf_op | source)
XLA Modules:
  0.0 311.8 jit_solution(2910430649509161215)
XLA Ops:
  0.9 9.9 %units.1 = (bf16[512,4224]{1,0:T(8,128)(2,1)}, bf16[512,4224]{1,0:T(8,128)(2,1)S(1)}, bf16[512,4224]{1,0:T(8,128)(2,1)S(1)}) custom-call(s32[2]{0:T(128)S(1)} %pad_add_fusion.info, bf16[512,8192]{1,0:T(8,128)(2,1)} %x_ref.1, bf16[512,128]{1,0:T(8,128)(2,1)S(1)} %fusion.tag_ref), custom_call_target="tpu_custom_call" | custom-call | flops 25165824 | bytes 20971520 | tf_op jit(solution)/shard_map/units/pallas_call | solution.py:85
  10.8 12.9 %collective-permute-start = (bf16[512,4224]{1,0:T(8,128)(2,1)}, bf16[512,4224]{1,0:T(8,128)(2,1)S(1)}, u32[]{:S(2)}, u32[]{:S(2)}) collective-permute-start(bf16[512,4224]{1,0:T(8,128)(2,1)} %get-tuple-element.35), channel_id=1, source_target_pairs={{1,255},{63,65},{0,192},{62,126},{61,125},{2,194},{65,63},{127,129... | collective-permute-start | bytes 12976136 | tf_op jit(solution)/shard_map/ppermute | solution.py:278
  23.8 3.3 %collective-permute-start.3 = (bf16[512,4224]{1,0:T(8,128)(2,1)}, bf16[512,4224]{1,0:T(8,128)(2,1)}, u32[]{:S(2)}, u32[]{:S(2)}) collective-permute-start(bf16[512,4224]{1,0:T(8,128)(2,1)} %get-tuple-element.35), channel_id=1, source_target_pairs={{0,2},{1,3},{2,4},{3,5},{4,6},{5,7},{6,8},{7,9},{8,10},{9,11},{10,... | collective-permute-start | bytes 12976136 | tf_op jit(solution)/shard_map/ppermute | solution.py:23
  28.0 1.3 collective-permute-start.2
  29.3 42.0 %collective-permute-done.odd = bf16[512,4224]{1,0:T(8,128)(2,1)S(1)} collective-permute-done((bf16[512,4224]{1,0:T(8,128)(2,1)}, bf16[512,4224]{1,0:T(8,128)(2,1)S(1)}, u32[]{:S(2)}, u32[]{:S(2)}) %collective-permute-start) | collective-permute-done | bytes 4325408 | tf_op jit(solution)/shard_map/ppermute | solution.py:278
  71.6 1.7 copy-done
  74.3 47.0 %collective-permute-done.2.after_in = bf16[512,4224]{1,0:T(8,128)(2,1)} collective-permute-done((bf16[512,4224]{1,0:T(8,128)(2,1)S(1)}, bf16[512,4224]{1,0:T(8,128)(2,1)}, u32[]{:S(2)}, u32[]{:S(2)}) %collective-permute-start.2) | collective-permute-done | bytes 4325408 | tf_op jit(solution)/shard_map/ppermute | solution.py:23
  121.3 42.8 %collective-permute-done.1.refs_0_ = bf16[512,4224]{1,0:T(8,128)(2,1)S(1)} collective-permute-done((bf16[512,4224]{1,0:T(8,128)(2,1)S(1)}, bf16[512,4224]{1,0:T(8,128)(2,1)S(1)}, u32[]{:S(2)}, u32[]{:S(2)}) %collective-permute-start.1) | collective-permute-done | bytes 4325408 | tf_op jit(solution)/shard_map/ppermute | solution.py:23
  164.2 2.0 copy-done.8
  166.2 2.0 copy-done.2
  169.4 5.3 %broadcast_select_fusion = bf16[512,4224]{1,0:T(8,128)(2,1)} fusion(bf16[512,4224]{1,0:T(8,128)(2,1)} %copy-done.1, bf16[512,4224]{1,0:T(8,128)(2,1)} %copy-done, pred[]{:T(512)S(6)} %eq.47), kind=kLoop, calls=%fused_computation | loop fusion | flops 2162688 | bytes 12976129 | tf_op jit(solution)/shard_map/jit(_where)/select_n | solution.py:290
  175.9 3.2 %merge.1 = (bf16[512,4224]{1,0:T(8,128)(2,1)}, bf16[512,4224]{1,0:T(8,128)(2,1)}) custom-call(s32[2]{0:T(128)S(1)} %pad_add_fusion.1.info, bf16[512,4224]{1,0:T(8,128)(2,1)S(1)} %bitcast.14, bf16[512,4224]{1,0:T(8,128)(2,1)S(1)} %bitcast.12, bf16[512,4224]{1,0:T(8,128)(2,1)} %collective-permute-done.2.after_in, ...), custom_call_target="tpu_custom_call", output_to_operand_aliasing={{0}: (3, {}), {1}: (4, {})} | custom-call | bytes 1048576 | tf_op jit(solution)/shard_map/merge/pallas_call | solution.py:223
  179.7 3.3 %collective-permute-start.12 = (bf16[512,4224]{1,0:T(8,128)(2,1)}, bf16[512,4224]{1,0:T(8,128)(2,1)}, u32[]{:S(2)}, u32[]{:S(2)}) collective-permute-start(bf16[512,4224]{1,0:T(8,128)(2,1)} %get-tuple-element.43.refs_3_), channel_id=1, source_target_pairs={{1,2},{3,4},{5,6},{7,8},{9,10},{11,12},{13,14},{15,16},{17,18},{19... | collective-permute-start | bytes 12976136 | tf_op jit(solution)/shard_map/ppermute | solution.py:23
  183.0 1.3 collective-permute-start.13
  184.3 9.8 %tiles.3 = (bf16[2,512,512]{2,1,0:T(8,128)(2,1)S(1)}, bf16[512,512]{1,0:T(8,128)(2,1)S(1)}, bf16[512,512]{1,0:T(8,128)(2,1)S(1)}) custom-call(s32[3]{0:T(128)S(1)} %broadcast_3_info.2.info, bf16[512,4224]{1,0:T(8,128)(2,1)} %copy-done.8, bf16[512,4224]{1,0:T(8,128)(2,1)} %collective-permute-done.6.refs_1_, bf16[512,4224]{1,0:T(8,128)(2,1)} %get-tuple-element.39.refs_2_), custom_call_target="tpu_custom_call" | custom-call | flops 4294967296 | bytes 12582912 | tf_op jit(solution)/shard_map/tiles/pallas_call | solution.py:179
  195.0 3.1 collective-permute-start.14
  198.3 2.1 copy-done.10
  200.7 13.7 %tiles.4 = (bf16[3,512,512]{2,1,0:T(8,128)(2,1)}, bf16[512,512]{1,0:T(8,128)(2,1)S(1)}, bf16[2,512,512]{2,1,0:T(8,128)(2,1)S(1)}) custom-call(s32[4]{0:T(128)S(1)} %pad_add_fusion.2.info, bf16[512,4224]{1,0:T(8,128)(2,1)} %copy-done.8, bf16[512,4224]{1,0:T(8,128)(2,1)} %copy-done.7, bf16[512,4224]{1,0:T(8,128)(2,1)} %copy-done.9, ...), custom_call_target="tpu_custom_call" | custom-call | bytes 1048576 | tf_op jit(solution)/shard_map/tiles/pallas_call | solution.py:179
  214.6 12.6 %collective-permute-done.7.near = bf16[2,512,512]{2,1,0:T(8,128)(2,1)S(1)} collective-permute-done((bf16[2,512,512]{2,1,0:T(8,128)(2,1)S(1)}, bf16[2,512,512]{2,1,0:T(8,128)(2,1)S(1)}, u32[]{:S(2)}, u32[]{:S(2)}) %collective-permute-start.7) | collective-permute-done | bytes 1048608 | tf_op jit(solution)/shard_map/ppermute | solution.py:23
  228.5 6.4 %collective-permute-done.13.refs_3_ = bf16[512,4224]{1,0:T(8,128)(2,1)} collective-permute-done((bf16[512,4224]{1,0:T(8,128)(2,1)}, bf16[512,4224]{1,0:T(8,128)(2,1)}, u32[]{:S(2)}, u32[]{:S(2)}) %collective-permute-start.13) | collective-permute-done | bytes 4325408 | tf_op jit(solution)/shard_map/ppermute | solution.py:23
  236.2 3.6 %collective-permute-start.18 = (bf16[2,512,512]{2,1,0:T(8,128)(2,1)}, bf16[2,512,512]{2,1,0:T(8,128)(2,1)}, u32[]{:S(2)}, u32[]{:S(2)}) collective-permute-start(bf16[2,512,512]{2,1,0:T(8,128)(2,1)} %pad_maximum_fusion.2), channel_id=1, source_target_pairs={{0,254},{1,255},{2,0},{3,1},{4,2},{5,3},{6,4},{7,5},{8,6},{9,7},{1... | collective-permute-start | bytes 3145736 | tf_op jit(solution)/shard_map/ppermute | solution.py:23
  240.9 7.9 %tiles.5 = (bf16[1,512,512]{2,1,0:T(8,128)(2,1)}, bf16[512,512]{1,0:T(8,128)(2,1)}) custom-call(s32[2]{0:T(128)S(1)} %pad_add_fusion.3.info, bf16[512,4224]{1,0:T(8,128)(2,1)} %copy-done.8, bf16[512,4224]{1,0:T(8,128)(2,1)} %copy-done.7, bf16[512,4224]{1,0:T(8,128)(2,1)} %collective-permute-done.12.refs_2_, ...), custom_call_target="tpu_custom_call" | custom-call | flops 2147483648 | bytes 8388608 | tf_op jit(solution)/shard_map/tiles/pallas_call | solution.py:179
  250.3 56.0 %collective-permute-done.15.far = bf16[1,512,512]{2,1,0:T(8,128)(2,1)} collective-permute-done((bf16[1,512,512]{2,1,0:T(8,128)(2,1)}, bf16[1,512,512]{2,1,0:T(8,128)(2,1)}, u32[]{:S(2)}, u32[]{:S(2)}) %collective-permute-start.15) | collective-permute-done | bytes 524320 | tf_op jit(solution)/shard_map/ppermute | solution.py:23
  307.6 4.2 %add_up.1 = bf16[6,512,512]{2,1,0:T(8,128)(2,1)} custom-call(s32[6]{0:T(128)S(1)} %broadcast_select_fusion.1.slots, bf16[2,512,512]{2,1,0:T(8,128)(2,1)S(1)} %copy-done.4, bf16[3,512,512]{2,1,0:T(8,128)(2,1)S(1)} %collective-permute-done.11.mid, bf16[1,512,512]{2,1,0:T(8,128)(2,1)} %collective-permute-done.15.far, ...), custom_call_target="tpu_custom_call" | custom-call | flops 1572864 | bytes 9437184 | tf_op jit(solution)/shard_map/add_up/pallas_call | solution.py:251
  (71 shorter events, 14.0 us)
Async XLA Ops:
  10.8 153.3 %copy-start.1 = (bf16[512,4224]{1,0:T(8,128)(2,1)}, bf16[512,4224]{1,0:T(8,128)(2,1)S(1)}, u32[]{:S(2)}) copy-start(bf16[512,4224]{1,0:T(8,128)(2,1)S(1)} %get-tuple-element.33) | copy-start | bytes 12976132
  10.8 60.5 %collective-permute-start = (bf16[512,4224]{1,0:T(8,128)(2,1)}, bf16[512,4224]{1,0:T(8,128)(2,1)S(1)}, u32[]{:S(2)}, u32[]{:S(2)}) collective-permute-start(bf16[512,4224]{1,0:T(8,128)(2,1)} %get-tuple-element.35), channel_id=1, source_target_pairs={{1,255},{63,65},{0,192},{62,126},{61,125},{2,194},{65,63},{127,129... | collective-permute-start | bytes 12976136 | tf_op jit(solution)/shard_map/ppermute | solution.py:278
  23.8 97.6 %collective-permute-start.3 = (bf16[512,4224]{1,0:T(8,128)(2,1)}, bf16[512,4224]{1,0:T(8,128)(2,1)}, u32[]{:S(2)}, u32[]{:S(2)}) collective-permute-start(bf16[512,4224]{1,0:T(8,128)(2,1)} %get-tuple-element.35), channel_id=1, source_target_pairs={{0,2},{1,3},{2,4},{3,5},{4,6},{5,7},{6,8},{7,9},{8,10},{9,11},{10,... | collective-permute-start | bytes 12976136 | tf_op jit(solution)/shard_map/ppermute | solution.py:23
  27.1 94.3 %collective-permute-start.4 = (bf16[512,4224]{1,0:T(8,128)(2,1)}, bf16[512,4224]{1,0:T(8,128)(2,1)S(1)}, u32[]{:S(2)}, u32[]{:S(2)}) collective-permute-start(bf16[512,4224]{1,0:T(8,128)(2,1)} %get-tuple-element.35), channel_id=1, source_target_pairs={{32,160},{33,225},{34,162},{160,32},{161,97},{162,34}} | collective-permute-start | bytes 12976136 | tf_op jit(solution)/shard_map/ppermute | solution.py:23
  28.0 93.3 %collective-permute-start.2 = (bf16[512,4224]{1,0:T(8,128)(2,1)S(1)}, bf16[512,4224]{1,0:T(8,128)(2,1)}, u32[]{:S(2)}, u32[]{:S(2)}) collective-permute-start(bf16[512,4224]{1,0:T(8,128)(2,1)S(1)} %get-tuple-element.34), channel_id=1, source_target_pairs={{2,0},{3,1},{4,2},{5,3},{6,4},{7,5},{8,6},{9,7},{10,8},{11,9},{12,... | collective-permute-start | bytes 12976136 | tf_op jit(solution)/shard_map/ppermute | solution.py:23
  71.4 92.8 %collective-permute-start.1 = (bf16[512,4224]{1,0:T(8,128)(2,1)S(1)}, bf16[512,4224]{1,0:T(8,128)(2,1)S(1)}, u32[]{:S(2)}, u32[]{:S(2)}) collective-permute-start(bf16[512,4224]{1,0:T(8,128)(2,1)S(1)} %get-tuple-element.33), channel_id=1, source_target_pairs={{0,128},{1,129},{2,130},{3,131},{4,132},{5,133},{6,134},{7,135},{8... | collective-permute-start | bytes 12976136 | tf_op jit(solution)/shard_map/ppermute | solution.py:23
  73.3 90.8 %collective-permute-start.5 = (bf16[512,4224]{1,0:T(8,128)(2,1)S(1)}, bf16[512,4224]{1,0:T(8,128)(2,1)S(1)}, u32[]{:S(2)}, u32[]{:S(2)}) collective-permute-start(bf16[512,4224]{1,0:T(8,128)(2,1)S(1)} %collective-permute-done.odd), channel_id=1, source_target_pairs={{0,62},{62,0},{64,126},{126,64},{128,190},{190,128},{192,254},{254... | collective-permute-start | bytes 12976136 | tf_op jit(solution)/shard_map/ppermute | solution.py:285
  121.3 42.8 %copy-start.7 = (bf16[512,4224]{1,0:T(8,128)(2,1)}, bf16[512,4224]{1,0:T(8,128)(2,1)S(1)}, u32[]{:S(2)}) copy-start(bf16[512,4224]{1,0:T(8,128)(2,1)S(1)} %collective-permute-done.4.refs_1_) | copy-start | bytes 12976132
  168.2 7.7 %collective-permute-start.6 = (bf16[512,4224]{1,0:T(8,128)(2,1)}, bf16[512,4224]{1,0:T(8,128)(2,1)}, u32[]{:S(2)}, u32[]{:S(2)}) collective-permute-start(bf16[512,4224]{1,0:T(8,128)(2,1)} %get-tuple-element.35), channel_id=1, source_target_pairs={{0,1},{1,0},{2,3},{3,2},{4,5},{5,4},{6,7},{7,6},{8,9},{9,8},{10,11... | collective-permute-start | bytes 12976136 | tf_op jit(solution)/shard_map/ppermute | solution.py:23
  168.3 26.6 %collective-permute-start.8 = (bf16[512,4224]{1,0:T(8,128)(2,1)}, bf16[512,4224]{1,0:T(8,128)(2,1)S(1)}, u32[]{:S(2)}, u32[]{:S(2)}) collective-permute-start(bf16[512,4224]{1,0:T(8,128)(2,1)} %copy-done.7), channel_id=1, source_target_pairs={{97,33},{225,161}} | collective-permute-start | bytes 12976136 | tf_op jit(solution)/shard_map/ppermute | solution.py:23
  179.1 18.9 %collective-permute-start.10 = (bf16[512,4224]{1,0:T(8,128)(2,1)}, bf16[512,4224]{1,0:T(8,128)(2,1)S(1)}, u32[]{:S(2)}, u32[]{:S(2)}) collective-permute-start(bf16[512,4224]{1,0:T(8,128)(2,1)} %get-tuple-element.43.refs_3_), channel_id=1, source_target_pairs={{0,1},{1,0},{2,3},{3,2},{4,5},{5,4},{6,7},{7,6},{8,9},{9,8},{10,11... | collective-permute-start | bytes 12976136 | tf_op jit(solution)/shard_map/ppermute | solution.py:23
  179.3 21.3 %collective-permute-start.9 = (bf16[512,4224]{1,0:T(8,128)(2,1)}, bf16[512,4224]{1,0:T(8,128)(2,1)}, u32[]{:S(2)}, u32[]{:S(2)}) collective-permute-start(bf16[512,4224]{1,0:T(8,128)(2,1)} %get-tuple-element.39.refs_2_), channel_id=1, source_target_pairs={{0,1},{1,0},{2,3},{3,2},{4,5},{5,4},{6,7},{7,6},{8,9},{9,8},{10,11... | collective-permute-start | bytes 12976136 | tf_op jit(solution)/shard_map/ppermute | solution.py:23
  179.7 48.8 %collective-permute-start.12 = (bf16[512,4224]{1,0:T(8,128)(2,1)}, bf16[512,4224]{1,0:T(8,128)(2,1)}, u32[]{:S(2)}, u32[]{:S(2)}) collective-permute-start(bf16[512,4224]{1,0:T(8,128)(2,1)} %get-tuple-element.43.refs_3_), channel_id=1, source_target_pairs={{1,2},{3,4},{5,6},{7,8},{9,10},{11,12},{13,14},{15,16},{17,18},{19... | collective-permute-start | bytes 12976136 | tf_op jit(solution)/shard_map/ppermute | solution.py:23
  183.0 51.8 %collective-permute-start.13 = (bf16[512,4224]{1,0:T(8,128)(2,1)}, bf16[512,4224]{1,0:T(8,128)(2,1)}, u32[]{:S(2)}, u32[]{:S(2)}) collective-permute-start(bf16[512,4224]{1,0:T(8,128)(2,1)} %get-tuple-element.39.refs_2_), channel_id=1, source_target_pairs={{2,1},{4,3},{6,5},{8,7},{10,9},{12,11},{14,13},{16,15},{18,17},{20... | collective-permute-start | bytes 12976136 | tf_op jit(solution)/shard_map/ppermute | solution.py:23
  195.0 46.0 %collective-permute-start.14 = (bf16[512,4224]{1,0:T(8,128)(2,1)}, bf16[512,4224]{1,0:T(8,128)(2,1)}, u32[]{:S(2)}, u32[]{:S(2)}) collective-permute-start(bf16[512,4224]{1,0:T(8,128)(2,1)} %broadcast_select_fusion), channel_id=1, source_target_pairs={{61,0},{2,63},{125,64},{66,127},{189,128},{130,191},{253,192},{194... | collective-permute-start | bytes 12976136 | tf_op jit(solution)/shard_map/ppermute | solution.py:303
  200.4 26.7 %collective-permute-start.7 = (bf16[2,512,512]{2,1,0:T(8,128)(2,1)S(1)}, bf16[2,512,512]{2,1,0:T(8,128)(2,1)S(1)}, u32[]{:S(2)}, u32[]{:S(2)}) collective-permute-start(bf16[2,512,512]{2,1,0:T(8,128)(2,1)S(1)} %get-tuple-element.40), channel_id=1, source_target_pairs={{0,128},{1,129},{2,130},{3,131},{4,132},{5,133},{6,134},{7,135},{8... | collective-permute-start | bytes 3145736 | tf_op jit(solution)/shard_map/ppermute | solution.py:23
  214.4 25.3 %copy-start.6 = (bf16[512,512]{1,0:T(8,128)(2,1)S(1)}, bf16[512,512]{1,0:T(8,128)(2,1)}, u32[]{:S(2)}) copy-start(bf16[512,512]{1,0:T(8,128)(2,1)} %copy-done.5) | copy-start | bytes 1572868
  228.1 6.9 %collective-permute-start.16 = (bf16[3,512,512]{2,1,0:T(8,128)(2,1)S(1)}, bf16[3,512,512]{2,1,0:T(8,128)(2,1)S(1)}, u32[]{:S(2)}, u32[]{:S(2)}) collective-permute-start(bf16[3,512,512]{2,1,0:T(8,128)(2,1)S(1)} %pad_maximum_fusion), channel_id=1, source_target_pairs={{0,1},{1,0},{2,3},{3,2},{4,5},{5,4},{6,7},{7,6},{8,9},{9,8},{10,11... | collective-permute-start | bytes 4718600 | tf_op jit(solution)/shard_map/ppermute | solution.py:23
  234.8 71.5 %collective-permute-start.11 = (bf16[3,512,512]{2,1,0:T(8,128)(2,1)}, bf16[3,512,512]{2,1,0:T(8,128)(2,1)S(1)}, u32[]{:S(2)}, u32[]{:S(2)}) collective-permute-start(bf16[3,512,512]{2,1,0:T(8,128)(2,1)} %get-tuple-element.44), channel_id=1, source_target_pairs={{0,128},{1,129},{2,130},{3,131},{4,132},{5,133},{6,134},{7,135},{8... | collective-permute-start | bytes 4718600 | tf_op jit(solution)/shard_map/ppermute | solution.py:23
  236.2 70.2 %collective-permute-start.18 = (bf16[2,512,512]{2,1,0:T(8,128)(2,1)}, bf16[2,512,512]{2,1,0:T(8,128)(2,1)}, u32[]{:S(2)}, u32[]{:S(2)}) collective-permute-start(bf16[2,512,512]{2,1,0:T(8,128)(2,1)} %pad_maximum_fusion.2), channel_id=1, source_target_pairs={{0,254},{1,255},{2,0},{3,1},{4,2},{5,3},{6,4},{7,5},{8,6},{9,7},{1... | collective-permute-start | bytes 3145736 | tf_op jit(solution)/shard_map/ppermute | solution.py:23
  240.8 65.5 %collective-permute-start.17 = (bf16[2,512,512]{2,1,0:T(8,128)(2,1)}, bf16[2,512,512]{2,1,0:T(8,128)(2,1)}, u32[]{:S(2)}, u32[]{:S(2)}) collective-permute-start(bf16[2,512,512]{2,1,0:T(8,128)(2,1)} %pad_maximum_fusion.1), channel_id=1, source_target_pairs={{0,2},{1,3},{2,4},{3,5},{4,6},{5,7},{6,8},{7,9},{8,10},{9,11},{10,... | collective-permute-start | bytes 3145736 | tf_op jit(solution)/shard_map/ppermute | solution.py:23
  240.9 9.4 %copy-start.12 = (s32[6]{0:T(128)S(1)}, s32[6]{0:T(128)}, u32[]{:S(2)}) copy-start(s32[6]{0:T(128)} %constant.94.clone) | copy-start | bytes 76
  248.8 57.6 %collective-permute-start.15 = (bf16[1,512,512]{2,1,0:T(8,128)(2,1)}, bf16[1,512,512]{2,1,0:T(8,128)(2,1)}, u32[]{:S(2)}, u32[]{:S(2)}) collective-permute-start(bf16[1,512,512]{2,1,0:T(8,128)(2,1)} %get-tuple-element.49), channel_id=1, source_target_pairs={{0,128},{1,129},{2,130},{3,131},{4,132},{5,133},{6,134},{7,135},{8... | collective-permute-start | bytes 1572872 | tf_op jit(solution)/shard_map/ppermute | solution.py:23
  249.6 56.7 %collective-permute-start.19 = (bf16[512,512]{1,0:T(8,128)(2,1)}, bf16[512,512]{1,0:T(8,128)(2,1)}, u32[]{:S(2)}, u32[]{:S(2)}) collective-permute-start(bf16[512,512]{1,0:T(8,128)(2,1)} %get-tuple-element.56), channel_id=1, source_target_pairs={{0,253},{1,4},{2,255},{3,6},{4,1},{5,8},{6,3},{7,10},{8,5},{9,12},... | collective-permute-start | bytes 1572872 | tf_op jit(solution)/shard_map/ppermute | solution.py:23
  (13 other events, 54.5 us)

commit v5 on v4

--- a/solution.py
+++ b/solution.py
@@ -15,6 +15,7 @@
 WIDE = HALF + TAG
 NSTEP = 256
 ROWS = 64
+PIECE = 512
 MIB = 1024 * 1024
 
 
@@ -57,26 +58,29 @@
 
 
 def unit_kernel(info, x_ref, tag_ref, keep_ref, other_ref, ahead_ref):
-    x = x_ref[...].astype(jnp.float32)
-    squares = jnp.sum(x * x, axis=1, keepdims=True)
-    unit = (x * (1.0 / jnp.sqrt(squares + 1e-06))).astype(jnp.bfloat16)
-    low, high = unit[:, :HALF], unit[:, HALF:]
-    tag = tag_ref[...]
-
-    def put(ref, half):
-        @pl.when(half == 0)
-        def _():
-            ref[:, :HALF] = low
-
-        @pl.when(half != 0)
-        def _():
-            ref[:, :HALF] = high
-
-        ref[:, HALF:] = tag
-
-    put(keep_ref, info[0])
-    put(other_ref, 1 - info[0])
-    put(ahead_ref, info[1])
+    same = info[0] == info[1]
+    starts = [pl.multiple_of(half * HALF, HALF) for half in (info[0], 1 - info[0])]
+
+    def some_rows(r, _):
+        span = pl.ds(pl.multiple_of(r * 16, 16), 16)
+        total = jnp.zeros((16, PIECE), jnp.float32)
+        for c in range(2 * HALF // PIECE):
+            x = x_ref[span, c * PIECE : (c + 1) * PIECE].astype(jnp.float32)
+            total += x * x
+        scale = 1.0 / jnp.sqrt(jnp.sum(total, axis=1, keepdims=True) + 1e-06)
+        for c in range(HALF // PIECE):
+            put = slice(c * PIECE, (c + 1) * PIECE)
+            own, rest = (
+                x_ref[span, pl.ds(start + c * PIECE, PIECE)].astype(jnp.float32) * scale for start in starts
+            )
+            keep_ref[span, put] = own.astype(jnp.bfloat16)
+            other_ref[span, put] = rest.astype(jnp.bfloat16)
+            ahead_ref[span, put] = jnp.where(same, own, rest).astype(jnp.bfloat16)
+        for ref in (keep_ref, other_ref, ahead_ref):
+            ref[span, HALF:] = tag_ref[span, :]
+        return 0
+
+    lax.fori_loop(0, ROWS // 16, some_rows, 0)
 
 
 def make_units(features, tags, own_half, ahead_half):

time: 312 us -> 313 us (level)
  no operation moved by 1% of the time
where the time goes in v5:
time: 313 us; the launch traced here: 312 us
  waiting for transfers between devices  208 us (66%)
  Pallas kernels  49.4 us (16%)
  starting transfers between devices  34.7 us (11%)
  local copies, waits for them, and re-layouts  11.2 us (4%)
  other arithmetic  8.79 us (3%)
    ppermute x17, waiting for transfers between devices, send(): return lax.ppermute(block, 'blk', pairs)  166 us
    ppermute x1, waiting for transfers between devices, local(): crossed_once = lax.ppermute(keep, 'blk', first)  42 us
    pallas_call x3, Pallas kernels, tiles(): pl.pallas_call(kernel, out_shape=outs, in_specs=[pl.BlockSpec(memory_spac...  31.5 us
    ppermute x17, starting transfers between devices, send(): return lax.ppermute(block, 'blk', pairs)  17.8 us
    ppermute x1, starting transfers between devices, local(): crossed_once = lax.ppermute(keep, 'blk', first)  12.9 us
    unnamed x34, local copies, waits for them, and re-layouts  11.2 us
    pallas_call x1, Pallas kernels, make_units(): pl.pallas_call(unit_kernel, out_shape=(out, out, out), grid_spec=pltpu.Pr...  10.5 us
  transfers between devices with their start and end apart: 20, of which 7 were waited for; matrix products, arithmetic and copies ran while one was open for 3% of the time, Pallas kernels for 11%

profile of v5, /device:TPU:1, one launch (start us, length us, event | category | flops | bytes accessed | tf_op | source)
XLA Modules:
  0.0 312.4 jit_solution(17055035036438455211)
XLA Ops:
  0.9 10.5 %units.1 = (bf16[512,4224]{1,0:T(8,128)(2,1)}, bf16[512,4224]{1,0:T(8,128)(2,1)S(1)}, bf16[512,4224]{1,0:T(8,128)(2,1)S(1)}) custom-call(s32[2]{0:T(128)S(1)} %pad_add_fusion.info, bf16[512,8192]{1,0:T(8,128)(2,1)} %x_ref.1, bf16[512,128]{1,0:T(8,128)(2,1)S(1)} %fusion.tag_ref), custom_call_target="tpu_custom_call" | custom-call | flops 25165824 | bytes 20971520 | tf_op jit(solution)/shard_map/units/pallas_call | solution.py:89
  11.4 12.9 %collective-permute-start = (bf16[512,4224]{1,0:T(8,128)(2,1)}, bf16[512,4224]{1,0:T(8,128)(2,1)S(1)}, u32[]{:S(2)}, u32[]{:S(2)}) collective-permute-start(bf16[512,4224]{1,0:T(8,128)(2,1)} %get-tuple-element.35), channel_id=1, source_target_pairs={{1,255},{63,65},{0,192},{62,126},{61,125},{2,194},{65,63},{127,129... | collective-permute-start | bytes 12976136 | tf_op jit(solution)/shard_map/ppermute | solution.py:282
  24.4 3.3 %collective-permute-start.3 = (bf16[512,4224]{1,0:T(8,128)(2,1)}, bf16[512,4224]{1,0:T(8,128)(2,1)}, u32[]{:S(2)}, u32[]{:S(2)}) collective-permute-start(bf16[512,4224]{1,0:T(8,128)(2,1)} %get-tuple-element.35), channel_id=1, source_target_pairs={{0,2},{1,3},{2,4},{3,5},{4,6},{5,7},{6,8},{7,9},{8,10},{9,11},{10,... | collective-permute-start | bytes 12976136 | tf_op jit(solution)/shard_map/ppermute | solution.py:24
  28.6 1.3 collective-permute-start.2
  29.9 42.0 %collective-permute-done.odd = bf16[512,4224]{1,0:T(8,128)(2,1)S(1)} collective-permute-done((bf16[512,4224]{1,0:T(8,128)(2,1)}, bf16[512,4224]{1,0:T(8,128)(2,1)S(1)}, u32[]{:S(2)}, u32[]{:S(2)}) %collective-permute-start) | collective-permute-done | bytes 4325408 | tf_op jit(solution)/shard_map/ppermute | solution.py:282
  72.2 1.7 copy-done
  74.9 47.0 %collective-permute-done.2.after_in = bf16[512,4224]{1,0:T(8,128)(2,1)} collective-permute-done((bf16[512,4224]{1,0:T(8,128)(2,1)S(1)}, bf16[512,4224]{1,0:T(8,128)(2,1)}, u32[]{:S(2)}, u32[]{:S(2)}) %collective-permute-start.2) | collective-permute-done | bytes 4325408 | tf_op jit(solution)/shard_map/ppermute | solution.py:24
  122.0 42.8 %collective-permute-done.1.refs_0_ = bf16[512,4224]{1,0:T(8,128)(2,1)S(1)} collective-permute-done((bf16[512,4224]{1,0:T(8,128)(2,1)S(1)}, bf16[512,4224]{1,0:T(8,128)(2,1)S(1)}, u32[]{:S(2)}, u32[]{:S(2)}) %collective-permute-start.1) | collective-permute-done | bytes 4325408 | tf_op jit(solution)/shard_map/ppermute | solution.py:24
  164.8 2.0 copy-done.8
  166.8 2.0 copy-done.2
  170.0 5.3 %broadcast_select_fusion = bf16[512,4224]{1,0:T(8,128)(2,1)} fusion(bf16[512,4224]{1,0:T(8,128)(2,1)} %copy-done.1, bf16[512,4224]{1,0:T(8,128)(2,1)} %copy-done, pred[]{:T(512)S(6)} %eq.47), kind=kLoop, calls=%fused_computation | loop fusion | flops 2162688 | bytes 12976129 | tf_op jit(solution)/shard_map/jit(_where)/select_n | solution.py:294
  176.5 3.2 %merge.1 = (bf16[512,4224]{1,0:T(8,128)(2,1)}, bf16[512,4224]{1,0:T(8,128)(2,1)}) custom-call(s32[2]{0:T(128)S(1)} %pad_add_fusion.1.info, bf16[512,4224]{1,0:T(8,128)(2,1)S(1)} %bitcast.14, bf16[512,4224]{1,0:T(8,128)(2,1)S(1)} %bitcast.12, bf16[512,4224]{1,0:T(8,128)(2,1)} %collective-permute-done.2.after_in, ...), custom_call_target="tpu_custom_call", output_to_operand_aliasing={{0}: (3, {}), {1}: (4, {})} | custom-call | bytes 1048576 | tf_op jit(solution)/shard_map/merge/pallas_call | solution.py:227
  180.3 3.3 %collective-permute-start.12 = (bf16[512,4224]{1,0:T(8,128)(2,1)}, bf16[512,4224]{1,0:T(8,128)(2,1)}, u32[]{:S(2)}, u32[]{:S(2)}) collective-permute-start(bf16[512,4224]{1,0:T(8,128)(2,1)} %get-tuple-element.43.refs_3_), channel_id=1, source_target_pairs={{1,2},{3,4},{5,6},{7,8},{9,10},{11,12},{13,14},{15,16},{17,18},{19... | collective-permute-start | bytes 12976136 | tf_op jit(solution)/shard_map/ppermute | solution.py:24
  183.6 1.3 collective-permute-start.13
  184.9 9.8 %tiles.3 = (bf16[2,512,512]{2,1,0:T(8,128)(2,1)S(1)}, bf16[512,512]{1,0:T(8,128)(2,1)S(1)}, bf16[512,512]{1,0:T(8,128)(2,1)S(1)}) custom-call(s32[3]{0:T(128)S(1)} %broadcast_3_info.2.info, bf16[512,4224]{1,0:T(8,128)(2,1)} %copy-done.8, bf16[512,4224]{1,0:T(8,128)(2,1)} %collective-permute-done.6.refs_1_, bf16[512,4224]{1,0:T(8,128)(2,1)} %get-tuple-element.39.refs_2_), custom_call_target="tpu_custom_call" | custom-call | flops 4294967296 | bytes 12582912 | tf_op jit(solution)/shard_map/tiles/pallas_call | solution.py:183
  195.5 3.1 collective-permute-start.14
  198.9 2.1 copy-done.10
  201.3 13.8 %tiles.4 = (bf16[3,512,512]{2,1,0:T(8,128)(2,1)}, bf16[512,512]{1,0:T(8,128)(2,1)S(1)}, bf16[2,512,512]{2,1,0:T(8,128)(2,1)S(1)}) custom-call(s32[4]{0:T(128)S(1)} %pad_add_fusion.2.info, bf16[512,4224]{1,0:T(8,128)(2,1)} %copy-done.8, bf16[512,4224]{1,0:T(8,128)(2,1)} %copy-done.7, bf16[512,4224]{1,0:T(8,128)(2,1)} %copy-done.9, ...), custom_call_target="tpu_custom_call" | custom-call | bytes 1048576 | tf_op jit(solution)/shard_map/tiles/pallas_call | solution.py:183
  215.2 12.5 %collective-permute-done.7.near = bf16[2,512,512]{2,1,0:T(8,128)(2,1)S(1)} collective-permute-done((bf16[2,512,512]{2,1,0:T(8,128)(2,1)S(1)}, bf16[2,512,512]{2,1,0:T(8,128)(2,1)S(1)}, u32[]{:S(2)}, u32[]{:S(2)}) %collective-permute-start.7) | collective-permute-done | bytes 1048608 | tf_op jit(solution)/shard_map/ppermute | solution.py:24
  229.1 6.4 %collective-permute-done.13.refs_3_ = bf16[512,4224]{1,0:T(8,128)(2,1)} collective-permute-done((bf16[512,4224]{1,0:T(8,128)(2,1)}, bf16[512,4224]{1,0:T(8,128)(2,1)}, u32[]{:S(2)}, u32[]{:S(2)}) %collective-permute-start.13) | collective-permute-done | bytes 4325408 | tf_op jit(solution)/shard_map/ppermute | solution.py:24
  236.8 3.6 %collective-permute-start.18 = (bf16[2,512,512]{2,1,0:T(8,128)(2,1)}, bf16[2,512,512]{2,1,0:T(8,128)(2,1)}, u32[]{:S(2)}, u32[]{:S(2)}) collective-permute-start(bf16[2,512,512]{2,1,0:T(8,128)(2,1)} %pad_maximum_fusion.2), channel_id=1, source_target_pairs={{0,254},{1,255},{2,0},{3,1},{4,2},{5,3},{6,4},{7,5},{8,6},{9,7},{1... | collective-permute-start | bytes 3145736 | tf_op jit(solution)/shard_map/ppermute | solution.py:24
  241.5 7.9 %tiles.5 = (bf16[1,512,512]{2,1,0:T(8,128)(2,1)}, bf16[512,512]{1,0:T(8,128)(2,1)}) custom-call(s32[2]{0:T(128)S(1)} %pad_add_fusion.3.info, bf16[512,4224]{1,0:T(8,128)(2,1)} %copy-done.8, bf16[512,4224]{1,0:T(8,128)(2,1)} %copy-done.7, bf16[512,4224]{1,0:T(8,128)(2,1)} %collective-permute-done.12.refs_2_, ...), custom_call_target="tpu_custom_call" | custom-call | flops 2147483648 | bytes 8388608 | tf_op jit(solution)/shard_map/tiles/pallas_call | solution.py:183
  250.9 56.0 %collective-permute-done.15.far = bf16[1,512,512]{2,1,0:T(8,128)(2,1)} collective-permute-done((bf16[1,512,512]{2,1,0:T(8,128)(2,1)}, bf16[1,512,512]{2,1,0:T(8,128)(2,1)}, u32[]{:S(2)}, u32[]{:S(2)}) %collective-permute-start.15) | collective-permute-done | bytes 524320 | tf_op jit(solution)/shard_map/ppermute | solution.py:24
  308.2 4.2 %add_up.1 = bf16[6,512,512]{2,1,0:T(8,128)(2,1)} custom-call(s32[6]{0:T(128)S(1)} %broadcast_select_fusion.1.slots, bf16[2,512,512]{2,1,0:T(8,128)(2,1)S(1)} %copy-done.4, bf16[3,512,512]{2,1,0:T(8,128)(2,1)S(1)} %collective-permute-done.11.mid, bf16[1,512,512]{2,1,0:T(8,128)(2,1)} %collective-permute-done.15.far, ...), custom_call_target="tpu_custom_call" | custom-call | flops 1572864 | bytes 9437184 | tf_op jit(solution)/shard_map/add_up/pallas_call | solution.py:255
  (71 shorter events, 14.1 us)
Async XLA Ops:
  11.4 153.3 %copy-start.1 = (bf16[512,4224]{1,0:T(8,128)(2,1)}, bf16[512,4224]{1,0:T(8,128)(2,1)S(1)}, u32[]{:S(2)}) copy-start(bf16[512,4224]{1,0:T(8,128)(2,1)S(1)} %get-tuple-element.33) | copy-start | bytes 12976132
  11.4 60.5 %collective-permute-start = (bf16[512,4224]{1,0:T(8,128)(2,1)}, bf16[512,4224]{1,0:T(8,128)(2,1)S(1)}, u32[]{:S(2)}, u32[]{:S(2)}) collective-permute-start(bf16[512,4224]{1,0:T(8,128)(2,1)} %get-tuple-element.35), channel_id=1, source_target_pairs={{1,255},{63,65},{0,192},{62,126},{61,125},{2,194},{65,63},{127,129... | collective-permute-start | bytes 12976136 | tf_op jit(solution)/shard_map/ppermute | solution.py:282
  24.4 97.6 %collective-permute-start.3 = (bf16[512,4224]{1,0:T(8,128)(2,1)}, bf16[512,4224]{1,0:T(8,128)(2,1)}, u32[]{:S(2)}, u32[]{:S(2)}) collective-permute-start(bf16[512,4224]{1,0:T(8,128)(2,1)} %get-tuple-element.35), channel_id=1, source_target_pairs={{0,2},{1,3},{2,4},{3,5},{4,6},{5,7},{6,8},{7,9},{8,10},{9,11},{10,... | collective-permute-start | bytes 12976136 | tf_op jit(solution)/shard_map/ppermute | solution.py:24
  27.7 94.3 %collective-permute-start.4 = (bf16[512,4224]{1,0:T(8,128)(2,1)}, bf16[512,4224]{1,0:T(8,128)(2,1)S(1)}, u32[]{:S(2)}, u32[]{:S(2)}) collective-permute-start(bf16[512,4224]{1,0:T(8,128)(2,1)} %get-tuple-element.35), channel_id=1, source_target_pairs={{32,160},{33,225},{34,162},{160,32},{161,97},{162,34}} | collective-permute-start | bytes 12976136 | tf_op jit(solution)/shard_map/ppermute | solution.py:24
  28.6 93.3 %collective-permute-start.2 = (bf16[512,4224]{1,0:T(8,128)(2,1)S(1)}, bf16[512,4224]{1,0:T(8,128)(2,1)}, u32[]{:S(2)}, u32[]{:S(2)}) collective-permute-start(bf16[512,4224]{1,0:T(8,128)(2,1)S(1)} %get-tuple-element.34), channel_id=1, source_target_pairs={{2,0},{3,1},{4,2},{5,3},{6,4},{7,5},{8,6},{9,7},{10,8},{11,9},{12,... | collective-permute-start | bytes 12976136 | tf_op jit(solution)/shard_map/ppermute | solution.py:24
  72.0 92.8 %collective-permute-start.1 = (bf16[512,4224]{1,0:T(8,128)(2,1)S(1)}, bf16[512,4224]{1,0:T(8,128)(2,1)S(1)}, u32[]{:S(2)}, u32[]{:S(2)}) collective-permute-start(bf16[512,4224]{1,0:T(8,128)(2,1)S(1)} %get-tuple-element.33), channel_id=1, source_target_pairs={{0,128},{1,129},{2,130},{3,131},{4,132},{5,133},{6,134},{7,135},{8... | collective-permute-start | bytes 12976136 | tf_op jit(solution)/shard_map/ppermute | solution.py:24
  74.0 90.8 %collective-permute-start.5 = (bf16[512,4224]{1,0:T(8,128)(2,1)S(1)}, bf16[512,4224]{1,0:T(8,128)(2,1)S(1)}, u32[]{:S(2)}, u32[]{:S(2)}) collective-permute-start(bf16[512,4224]{1,0:T(8,128)(2,1)S(1)} %collective-permute-done.odd), channel_id=1, source_target_pairs={{0,62},{62,0},{64,126},{126,64},{128,190},{190,128},{192,254},{254... | collective-permute-start | bytes 12976136 | tf_op jit(solution)/shard_map/ppermute | solution.py:289
  121.9 42.8 %copy-start.7 = (bf16[512,4224]{1,0:T(8,128)(2,1)}, bf16[512,4224]{1,0:T(8,128)(2,1)S(1)}, u32[]{:S(2)}) copy-start(bf16[512,4224]{1,0:T(8,128)(2,1)S(1)} %collective-permute-done.4.refs_1_) | copy-start | bytes 12976132
  168.8 7.7 %collective-permute-start.6 = (bf16[512,4224]{1,0:T(8,128)(2,1)}, bf16[512,4224]{1,0:T(8,128)(2,1)}, u32[]{:S(2)}, u32[]{:S(2)}) collective-permute-start(bf16[512,4224]{1,0:T(8,128)(2,1)} %get-tuple-element.35), channel_id=1, source_target_pairs={{0,1},{1,0},{2,3},{3,2},{4,5},{5,4},{6,7},{7,6},{8,9},{9,8},{10,11... | collective-permute-start | bytes 12976136 | tf_op jit(solution)/shard_map/ppermute | solution.py:24
  168.9 26.6 %collective-permute-start.8 = (bf16[512,4224]{1,0:T(8,128)(2,1)}, bf16[512,4224]{1,0:T(8,128)(2,1)S(1)}, u32[]{:S(2)}, u32[]{:S(2)}) collective-permute-start(bf16[512,4224]{1,0:T(8,128)(2,1)} %copy-done.7), channel_id=1, source_target_pairs={{97,33},{225,161}} | collective-permute-start | bytes 12976136 | tf_op jit(solution)/shard_map/ppermute | solution.py:24
  179.7 18.9 %collective-permute-start.10 = (bf16[512,4224]{1,0:T(8,128)(2,1)}, bf16[512,4224]{1,0:T(8,128)(2,1)S(1)}, u32[]{:S(2)}, u32[]{:S(2)}) collective-permute-start(bf16[512,4224]{1,0:T(8,128)(2,1)} %get-tuple-element.43.refs_3_), channel_id=1, source_target_pairs={{0,1},{1,0},{2,3},{3,2},{4,5},{5,4},{6,7},{7,6},{8,9},{9,8},{10,11... | collective-permute-start | bytes 12976136 | tf_op jit(solution)/shard_map/ppermute | solution.py:24
  179.9 21.3 %collective-permute-start.9 = (bf16[512,4224]{1,0:T(8,128)(2,1)}, bf16[512,4224]{1,0:T(8,128)(2,1)}, u32[]{:S(2)}, u32[]{:S(2)}) collective-permute-start(bf16[512,4224]{1,0:T(8,128)(2,1)} %get-tuple-element.39.refs_2_), channel_id=1, source_target_pairs={{0,1},{1,0},{2,3},{3,2},{4,5},{5,4},{6,7},{7,6},{8,9},{9,8},{10,11... | collective-permute-start | bytes 12976136 | tf_op jit(solution)/shard_map/ppermute | solution.py:24
  180.3 48.7 %collective-permute-start.12 = (bf16[512,4224]{1,0:T(8,128)(2,1)}, bf16[512,4224]{1,0:T(8,128)(2,1)}, u32[]{:S(2)}, u32[]{:S(2)}) collective-permute-start(bf16[512,4224]{1,0:T(8,128)(2,1)} %get-tuple-element.43.refs_3_), channel_id=1, source_target_pairs={{1,2},{3,4},{5,6},{7,8},{9,10},{11,12},{13,14},{15,16},{17,18},{19... | collective-permute-start | bytes 12976136 | tf_op jit(solution)/shard_map/ppermute | solution.py:24
  183.6 51.8 %collective-permute-start.13 = (bf16[512,4224]{1,0:T(8,128)(2,1)}, bf16[512,4224]{1,0:T(8,128)(2,1)}, u32[]{:S(2)}, u32[]{:S(2)}) collective-permute-start(bf16[512,4224]{1,0:T(8,128)(2,1)} %get-tuple-element.39.refs_2_), channel_id=1, source_target_pairs={{2,1},{4,3},{6,5},{8,7},{10,9},{12,11},{14,13},{16,15},{18,17},{20... | collective-permute-start | bytes 12976136 | tf_op jit(solution)/shard_map/ppermute | solution.py:24
  195.5 46.0 %collective-permute-start.14 = (bf16[512,4224]{1,0:T(8,128)(2,1)}, bf16[512,4224]{1,0:T(8,128)(2,1)}, u32[]{:S(2)}, u32[]{:S(2)}) collective-permute-start(bf16[512,4224]{1,0:T(8,128)(2,1)} %broadcast_select_fusion), channel_id=1, source_target_pairs={{61,0},{2,63},{125,64},{66,127},{189,128},{130,191},{253,192},{194... | collective-permute-start | bytes 12976136 | tf_op jit(solution)/shard_map/ppermute | solution.py:307
  201.0 26.7 %collective-permute-start.7 = (bf16[2,512,512]{2,1,0:T(8,128)(2,1)S(1)}, bf16[2,512,512]{2,1,0:T(8,128)(2,1)S(1)}, u32[]{:S(2)}, u32[]{:S(2)}) collective-permute-start(bf16[2,512,512]{2,1,0:T(8,128)(2,1)S(1)} %get-tuple-element.40), channel_id=1, source_target_pairs={{0,128},{1,129},{2,130},{3,131},{4,132},{5,133},{6,134},{7,135},{8... | collective-permute-start | bytes 3145736 | tf_op jit(solution)/shard_map/ppermute | solution.py:24
  215.0 25.3 %copy-start.6 = (bf16[512,512]{1,0:T(8,128)(2,1)S(1)}, bf16[512,512]{1,0:T(8,128)(2,1)}, u32[]{:S(2)}) copy-start(bf16[512,512]{1,0:T(8,128)(2,1)} %copy-done.5) | copy-start | bytes 1572868
  228.7 6.9 %collective-permute-start.16 = (bf16[3,512,512]{2,1,0:T(8,128)(2,1)S(1)}, bf16[3,512,512]{2,1,0:T(8,128)(2,1)S(1)}, u32[]{:S(2)}, u32[]{:S(2)}) collective-permute-start(bf16[3,512,512]{2,1,0:T(8,128)(2,1)S(1)} %pad_maximum_fusion), channel_id=1, source_target_pairs={{0,1},{1,0},{2,3},{3,2},{4,5},{5,4},{6,7},{7,6},{8,9},{9,8},{10,11... | collective-permute-start | bytes 4718600 | tf_op jit(solution)/shard_map/ppermute | solution.py:24
  235.4 71.5 %collective-permute-start.11 = (bf16[3,512,512]{2,1,0:T(8,128)(2,1)}, bf16[3,512,512]{2,1,0:T(8,128)(2,1)S(1)}, u32[]{:S(2)}, u32[]{:S(2)}) collective-permute-start(bf16[3,512,512]{2,1,0:T(8,128)(2,1)} %get-tuple-element.44), channel_id=1, source_target_pairs={{0,128},{1,129},{2,130},{3,131},{4,132},{5,133},{6,134},{7,135},{8... | collective-permute-start | bytes 4718600 | tf_op jit(solution)/shard_map/ppermute | solution.py:24
  236.8 70.2 %collective-permute-start.18 = (bf16[2,512,512]{2,1,0:T(8,128)(2,1)}, bf16[2,512,512]{2,1,0:T(8,128)(2,1)}, u32[]{:S(2)}, u32[]{:S(2)}) collective-permute-start(bf16[2,512,512]{2,1,0:T(8,128)(2,1)} %pad_maximum_fusion.2), channel_id=1, source_target_pairs={{0,254},{1,255},{2,0},{3,1},{4,2},{5,3},{6,4},{7,5},{8,6},{9,7},{1... | collective-permute-start | bytes 3145736 | tf_op jit(solution)/shard_map/ppermute | solution.py:24
  241.5 65.5 %collective-permute-start.17 = (bf16[2,512,512]{2,1,0:T(8,128)(2,1)}, bf16[2,512,512]{2,1,0:T(8,128)(2,1)}, u32[]{:S(2)}, u32[]{:S(2)}) collective-permute-start(bf16[2,512,512]{2,1,0:T(8,128)(2,1)} %pad_maximum_fusion.1), channel_id=1, source_target_pairs={{0,2},{1,3},{2,4},{3,5},{4,6},{5,7},{6,8},{7,9},{8,10},{9,11},{10,... | collective-permute-start | bytes 3145736 | tf_op jit(solution)/shard_map/ppermute | solution.py:24
  241.5 9.4 %copy-start.12 = (s32[6]{0:T(128)S(1)}, s32[6]{0:T(128)}, u32[]{:S(2)}) copy-start(s32[6]{0:T(128)} %constant.94.clone) | copy-start | bytes 76
  249.4 57.5 %collective-permute-start.15 = (bf16[1,512,512]{2,1,0:T(8,128)(2,1)}, bf16[1,512,512]{2,1,0:T(8,128)(2,1)}, u32[]{:S(2)}, u32[]{:S(2)}) collective-permute-start(bf16[1,512,512]{2,1,0:T(8,128)(2,1)} %get-tuple-element.49), channel_id=1, source_target_pairs={{0,128},{1,129},{2,130},{3,131},{4,132},{5,133},{6,134},{7,135},{8... | collective-permute-start | bytes 1572872 | tf_op jit(solution)/shard_map/ppermute | solution.py:24
  250.2 56.7 %collective-permute-start.19 = (bf16[512,512]{1,0:T(8,128)(2,1)}, bf16[512,512]{1,0:T(8,128)(2,1)}, u32[]{:S(2)}, u32[]{:S(2)}) collective-permute-start(bf16[512,512]{1,0:T(8,128)(2,1)} %get-tuple-element.56), channel_id=1, source_target_pairs={{0,253},{1,4},{2,255},{3,6},{4,1},{5,8},{6,3},{7,10},{8,5},{9,12},... | collective-permute-start | bytes 1572872 | tf_op jit(solution)/shard_map/ppermute | solution.py:24
  (13 other events, 54.5 us)
